TPU v7x, 32 devices: a whole 2x2x4 slice. The times are simulated.
32 devices in a mesh: section: 2 (over x), dp: 4 (over y, core), tensor: 4 (over z).
Axes of the slice: x: 2, y: 2, z: 4, core: 2. Of those that a mesh axis runs over, the one named last changes fastest.
Arguments:
- inputs: bfloat16 [2, 4352, 768], P(None, ('dp', 'tensor')), may hold values from -6 to 6
- cotangent: bfloat16 [2, 4352, 768], P(None, ('dp', 'tensor')), may hold values from -6 to 6
- lengths: int32 [2, 4, 3], P(None, 'dp'), may hold values from 1 to 1024, as said below
- routes: int32 [2, 2, 4352, 1], P('section', None, 'dp'), may hold values from 0 to 3; in each aligned block of 1088 rows (0 to 1087, 1088 to 2175, ..., all dimensions but the last counted through in order) at most 544 rows name the same one
- attn_gain: bfloat16 [2, 768], P('section', 'dp'), may hold values from 0.5 to 1.5
- moe_gain: bfloat16 [2, 768], P('section', 'dp'), may hold values from 0.5 to 1.5
- qkv_weight: bfloat16 [2, 768, 3, 768], P('section', 'dp', None, 'tensor'), may hold values from -0.078125 to 0.078125
- out_weight: bfloat16 [2, 768, 768], P('section', 'dp', 'tensor'), may hold values from -3.5 to 3.5
- bias_table: bfloat16 [2, 32, 12], P('section', 'dp', 'tensor'), may hold values from -4 to 4
- router: bfloat16 [2, 768, 4], P('section', 'dp'), may hold values from -0.15625 to 0.15625
- expert_up: bfloat16 [2, 4, 768, 3072], P('section', 'dp', None, 'tensor'), may hold values from -0.21875 to 0.21875
- expert_down: bfloat16 [2, 4, 3072, 768], P('section', 'dp', 'tensor'), may hold values from -0.4375 to 0.4375
Outputs:
- layer_outputs: bfloat16 [2, 2, 4352, 768], P('section', None, ('dp', 'tensor'))
- input_grads: bfloat16 [2, 2, 4352, 768], P('section', None, ('dp', 'tensor'))
- attn_gain_grad: float32 [2, 768], P('section', 'dp')
- moe_gain_grad: float32 [2, 768], P('section', 'dp')
- qkv_grad: float32 [2, 768, 3, 768], P('section', 'dp', None, 'tensor')
- out_grad: float32 [2, 768, 768], P('section', 'dp', 'tensor')
- bias_grad: float32 [2, 32, 12], P('section', 'dp', 'tensor')
- router_grad: float32 [2, 768, 4], P('section', 'dp')
- up_grad: float32 [2, 4, 768, 3072], P('section', 'dp', None, 'tensor')
- down_grad: float32 [2, 4, 3072, 768], P('section', 'dp', 'tensor')
Inputs may be any that keep to these rules, and one draw needn't show every extreme that they name: The 3 lengths of one group and micro-batch sum to 1088; the first of them is 1024. `routes`: within the 1088 tokens of one group, micro-batch and layer (aligned blocks of 1088 rows), at most 544 name one expert, and in some blocks an expert is named by exactly 544.
All inputs are finite; a program needn't handle non-finite values.
Results may differ from a plain program's by a relative error of at most 0.025.
Values may be sent and summed in bfloat16 or wider, within the bound.
A program may use at most 448 MiB of HBM per device.

v0:
```python
import jax
import jax.numpy as jnp
import numpy as np
from jax import lax
from jax.sharding import PartitionSpec as P

LONG = 1024


EPSILON = 1e-06
HIGHEST = lax.Precision.HIGHEST
TILE = 128
THRESHOLDS = np.array([12, 16, 23, 32, 46, 64, 91], dtype=np.int32)


def bucket_of(distance):
    magnitude = jnp.abs(distance)
    far_part = 8 + jnp.sum(
        (magnitude[..., None] >= jnp.asarray(THRESHOLDS)).astype(jnp.int32), axis=-1
    )
    nearby = jnp.where(magnitude < 8, magnitude, far_part)
    return nearby + 16 * (distance > 0).astype(jnp.int32)


def rms_apply(values, norm_gain):
    return (
        values * lax.rsqrt(jnp.mean(values * values, axis=-1, keepdims=True) + EPSILON) * norm_gain
    )


def gelu_apply(values):
    return jax.nn.gelu(values, approximate=True)


def gather_rows(piece):
    return lax.all_gather(piece, "tensor", axis=0, tiled=True)


def sum_rows(piece):
    return lax.psum_scatter(
        piece.astype(jnp.bfloat16), "tensor", scatter_dimension=0, tiled=True
    ).astype(jnp.float32)


def exchange(piece):
    return lax.all_to_all(piece, "dp", split_axis=0, concat_axis=0, tiled=True)


def swap_section(piece):
    return lax.ppermute(piece, "section", [(0, 1), (1, 0)])


def to_second(piece):
    return lax.ppermute(piece, "section", [(0, 1)])


def to_first(piece):
    return lax.ppermute(piece, "section", [(1, 0)])


def band_buckets():
    place = jnp.arange(TILE, dtype=jnp.int32)
    offset = (jnp.arange(3, dtype=jnp.int32) - 1) * TILE
    return bucket_of(offset[:, None, None] + place[None, None, :] - place[None, :, None])


def far_buckets():
    far = bucket_of(jnp.array([-TILE - 1, TILE + 1], dtype=jnp.int32))
    return far[0], far[1]


def relative_bias(rel_table):
    bucket_count, head_count = rel_table.shape
    buckets = band_buckets()
    table = rel_table.astype(jnp.float32).T
    choose = buckets[None, None] == jnp.arange(bucket_count, dtype=jnp.int32)[
        None, :, None, None, None
    ]
    band = jnp.sum(jnp.where(choose, table[:, :, None, None, None], 0.0), axis=1)
    band = band.astype(jnp.bfloat16)
    below, above = far_buckets()
    blocks = LONG // TILE
    shape = (head_count, TILE, (blocks - 2) * TILE)

    def far(number):
        value = jnp.sum(
            jnp.where(
                jnp.arange(bucket_count, dtype=jnp.int32)[None, :] == number, table, 0.0
            ),
            axis=1,
        ).astype(jnp.bfloat16)
        return jnp.broadcast_to(value[:, None, None], shape)

    strip = jnp.concatenate([far(below), band[:, 0], band[:, 1], band[:, 2], far(above)], axis=2)
    rows = [
        strip[:, :, (blocks - 1 - block) * TILE : (2 * blocks - 1 - block) * TILE]
        for block in range(blocks)
    ]
    return jnp.concatenate(rows, axis=1)


def bias_sums(head_grad, tail_grad, bucket_count):
    blocks = LONG // TILE
    tail = tail_grad.shape[1]

    def tile(row, column):
        return head_grad[
            :, row * TILE : (row + 1) * TILE, column * TILE : (column + 1) * TILE
        ].astype(jnp.float32)

    left = sum(tile(block, block - 1) for block in range(1, blocks))
    middle = sum(tile(block, block) for block in range(blocks))
    right = sum(tile(block, block + 1) for block in range(blocks - 1))
    middle = middle + jnp.pad(
        tail_grad.astype(jnp.float32), ((0, 0), (0, TILE - tail), (0, TILE - tail))
    )
    band = jnp.stack([left, middle, right], axis=1)
    numbers = jnp.arange(bucket_count, dtype=jnp.int32)
    choose = band_buckets()[None] == numbers[:, None, None, None]
    table = jnp.sum(jnp.where(choose[:, None], band[None], 0.0), axis=(2, 3, 4))
    block_of = jnp.arange(LONG, dtype=jnp.int32) // TILE
    apart = block_of[None, :] - block_of[:, None]
    wide = head_grad.astype(jnp.float32)
    low_sum = jnp.sum(jnp.where((apart <= -2)[None], wide, 0.0), axis=(1, 2))
    high_sum = jnp.sum(jnp.where((apart >= 2)[None], wide, 0.0), axis=(1, 2))
    below, above = far_buckets()
    table = table + jnp.where((numbers == below)[:, None], low_sum[None], 0.0)
    return table + jnp.where((numbers == above)[:, None], high_sum[None], 0.0)


def attend_scores(packed, rel_bias, allowed):
    scores = (
        jnp.einsum("qhe,khe->hqk", packed[:, 0], packed[:, 1], preferred_element_type=jnp.float32)
        + rel_bias
    )
    if allowed is None:
        return scores
    return jnp.where(allowed[None], scores, -1000000000.0)


def attend_forward(packed, rel_bias, allowed):
    scores = attend_scores(packed, rel_bias, allowed)
    row_max = jnp.max(scores, axis=-1, keepdims=True)
    expsum = jnp.exp(scores - row_max)
    total = jnp.sum(expsum, axis=-1, keepdims=True)
    chances = expsum / total
    log_total = row_max[..., 0] + jnp.log(total[..., 0])
    blended = jnp.einsum(
        "hqk,khe->qhe",
        chances.astype(jnp.bfloat16),
        packed[:, 2],
        preferred_element_type=jnp.float32,
    )
    return (blended.astype(jnp.bfloat16), log_total)


def attend_backward(packed, rel_bias, allowed, log_total, grad_blend):
    scores = attend_scores(packed, rel_bias, allowed)
    chances = jnp.exp(scores - log_total[..., None])
    grad_chance = jnp.einsum(
        "qhe,khe->hqk", grad_blend, packed[:, 2], preferred_element_type=jnp.float32
    )
    inner = jnp.sum(chances * grad_chance, axis=-1, keepdims=True)
    grad_score = (chances * (grad_chance - inner)).astype(jnp.bfloat16)
    grad_query = jnp.einsum(
        "hqk,khe->qhe", grad_score, packed[:, 1], preferred_element_type=jnp.float32
    )
    grad_key = jnp.einsum(
        "hqk,qhe->khe", grad_score, packed[:, 0], preferred_element_type=jnp.float32
    )
    grad_value = jnp.einsum(
        "hqk,qhe->khe", chances.astype(jnp.bfloat16), grad_blend, preferred_element_type=jnp.float32
    )
    grad_packed = jnp.stack([grad_query, grad_key, grad_value], axis=1).astype(jnp.bfloat16)
    return (grad_packed, grad_score)


def split_forward(packed, rel_bias, allowed):
    tail = packed.shape[0] - LONG
    head_blend, head_log = attend_forward(packed[:LONG], rel_bias, None)
    tail_blend, tail_log = attend_forward(packed[LONG:], rel_bias[:, :tail, :tail], allowed)
    return (jnp.concatenate([head_blend, tail_blend], axis=0), (head_log, tail_log))


def split_backward(packed, rel_bias, allowed, logs, grad_blend, bucket_count):
    tail = packed.shape[0] - LONG
    head_grad, head_scores = attend_backward(
        packed[:LONG], rel_bias, None, logs[0], grad_blend[:LONG]
    )
    tail_grad, tail_scores = attend_backward(
        packed[LONG:], rel_bias[:, :tail, :tail], allowed, logs[1], grad_blend[LONG:]
    )
    grad_table = bias_sums(head_scores, tail_scores, bucket_count)
    return (jnp.concatenate([head_grad, tail_grad], axis=0), grad_table)


def route_target(route_ids, experts, capacity):
    rows = route_ids.shape[0]
    choose = route_ids[:, None] == jnp.arange(experts, dtype=jnp.int32)[None, :]
    place = jnp.arange(rows, dtype=jnp.int32)
    earlier = (place[:, None] >= place[None, :]).astype(jnp.bfloat16)
    counted = jnp.dot(earlier, choose.astype(jnp.bfloat16), preferred_element_type=jnp.float32)
    slot = jnp.sum(jnp.where(choose, counted, 0.0), axis=1).astype(jnp.int32) - 1
    return route_ids * capacity + slot


def body(
    inputs,
    cotangent,
    lengths,
    routes,
    attn_gain,
    moe_gain,
    qkv_weight,
    out_weight,
    bias_table,
    router,
    expert_up,
    expert_down,
):
    section_pos = lax.axis_index("section")
    tensor_pos = lax.axis_index("tensor")
    tensor_count = lax.axis_size("tensor")
    dp_count = lax.axis_size("dp")
    batches, local_rows, model_dim = inputs.shape
    layers = lax.axis_size("section")
    group_rows = local_rows * tensor_count
    experts = router.shape[-1]
    capacity = 2 * group_rows // experts
    slots = capacity * experts
    assert batches == layers == 2 and expert_up.shape[1] == 1 and experts == dp_count
    first = section_pos == 0
    part = model_dim // dp_count
    head_feats = qkv_weight.shape[3]
    bucket_part, head_count = bias_table.shape[1:]
    bucket_count = bucket_part * dp_count
    head_dim = head_feats // head_count
    packed_feats = 3 * head_feats

    small = jnp.concatenate(
        [attn_gain[0], moe_gain[0], router[0].reshape(-1), bias_table[0].reshape(-1)]
    )
    smalls = lax.all_gather(small, ("section", "dp"), axis=0).reshape(layers, dp_count, -1)
    large = jnp.concatenate([qkv_weight[0].reshape(part, packed_feats), out_weight[0]], axis=1)
    larges = lax.all_gather(large, ("section", "dp"), axis=0, tiled=True)
    larges = larges.reshape(layers, model_dim, -1)
    all_routes = lax.all_gather(routes, "section", axis=0, tiled=True)
    other_up = swap_section(expert_up[0, 0])
    other_down = swap_section(expert_down[0, 0])
    up_mats = (
        jnp.where(first, expert_up[0, 0], other_up),
        jnp.where(first, other_up, expert_up[0, 0]),
    )
    down_mats = (
        jnp.where(first, expert_down[0, 0], other_down),
        jnp.where(first, other_down, expert_down[0, 0]),
    )

    seq_ends = jnp.cumsum(lax.dynamic_index_in_dim(lengths[:, 0], section_pos, 0, keepdims=False))
    places = jnp.arange(LONG, group_rows, dtype=jnp.int32)
    segment = jnp.sum((places[:, None] >= seq_ends[None, :]).astype(jnp.int32), axis=-1)
    allowed = segment[:, None] == segment[None, :]
    places_all = jnp.arange(slots, dtype=jnp.int32)

    def layer_setup(layer):
        route_ids = lax.dynamic_index_in_dim(all_routes[layer], section_pos, 0, keepdims=False)[:, 0]
        target = route_target(route_ids, experts, capacity)
        own_route = lax.dynamic_slice_in_dim(route_ids, tensor_pos * local_rows, local_rows)
        own_choose = (
            own_route[:, None] == jnp.arange(experts, dtype=jnp.int32)[None, :]
        ).astype(jnp.float32)
        scales = smalls[layer]
        attn_scale = scales[:, :part].reshape(-1).astype(jnp.float32)
        moe_scale = scales[:, part : 2 * part].reshape(-1).astype(jnp.float32)
        router_end = (2 + experts) * part
        router_mat = scales[:, 2 * part : router_end].reshape(model_dim, experts)
        rel_table = scales[:, router_end:].reshape(bucket_count, head_count)
        qkv_mat = larges[layer][:, :packed_feats]
        out_mat = larges[layer][:, packed_feats:]
        rel_bias = relative_bias(rel_table)
        return (target, own_choose, attn_scale, moe_scale, router_mat, qkv_mat, out_mat, rel_bias)

    def to_experts(own_rows, target):
        chosen = (places_all[:, None] == target[None, :]).astype(jnp.bfloat16)
        outgoing = jnp.dot(
            chosen, gather_rows(own_rows), preferred_element_type=jnp.float32
        ).astype(jnp.bfloat16)
        return exchange(outgoing.reshape(experts, capacity, model_dim)).reshape(-1, model_dim)

    def from_experts(produced, target):
        produced = produced.astype(jnp.bfloat16).reshape(experts, capacity, model_dim)
        returned = exchange(produced).reshape(slots, model_dim)
        chosen = (target[:, None] == places_all[None, :]).astype(jnp.bfloat16)
        own = jnp.dot(chosen, returned, preferred_element_type=jnp.float32)
        return sum_rows(own)

    def layer_forward(layer_in, setting, up_mat, down_mat):
        target, own_choose, attn_scale, moe_scale, router_mat, qkv_mat, out_mat, rel_bias = setting
        residual = layer_in.astype(jnp.float32)
        normed = rms_apply(residual, attn_scale).astype(jnp.bfloat16)
        normed_full = gather_rows(normed)
        packed = jnp.dot(normed_full, qkv_mat, preferred_element_type=jnp.float32)
        packed = packed.astype(jnp.bfloat16).reshape(group_rows, 3, head_count, head_dim)
        packed, up_mat, down_mat = lax.optimization_barrier((packed, up_mat, down_mat))
        blended, logs = split_forward(packed, rel_bias, allowed)
        attn_full = lax.dot_general(
            blended.reshape(group_rows, -1),
            out_mat,
            (((1,), (1,)), ((), ())),
            preferred_element_type=jnp.float32,
        )
        middle = residual + sum_rows(attn_full)
        branch = rms_apply(middle, moe_scale).astype(jnp.bfloat16)
        logits = jnp.dot(branch, router_mat, preferred_element_type=jnp.float32)
        received = to_experts(branch, target)
        pre_act = jnp.dot(received, up_mat, preferred_element_type=jnp.float32)
        hidden = gelu_apply(pre_act).astype(jnp.bfloat16)
        produced = jnp.dot(hidden, down_mat, preferred_element_type=jnp.float32)
        own_out = from_experts(produced, target).astype(jnp.bfloat16)
        chances = jax.nn.softmax(logits, axis=-1)
        gate_value = jnp.sum(chances * own_choose, axis=-1)
        result = (middle + gate_value[:, None] * own_out.astype(jnp.float32)).astype(jnp.bfloat16)
        stored = (
            residual,
            normed_full,
            packed,
            logs,
            blended,
            middle,
            branch,
            logits,
            own_out,
            received,
            pre_act,
            hidden,
        )
        return (result, stored)

    def layer_backward(grad_in, setting, stored, up_mat, down_mat, send, arrived):
        target, own_choose, attn_scale, moe_scale, router_mat, qkv_mat, out_mat, rel_bias = setting
        (
            residual,
            normed_full,
            packed,
            logs,
            blended,
            middle,
            branch,
            logits,
            own_out,
            received,
            pre_act,
            hidden,
        ) = stored
        grad_out = grad_in.astype(jnp.float32)

        def gate_of(logit_rows):
            return jnp.sum(jax.nn.softmax(logit_rows, axis=-1) * own_choose, axis=-1)

        gate_value, gate_pull = jax.vjp(gate_of, logits)
        grad_gate = jnp.sum(grad_out * own_out.astype(jnp.float32), axis=-1)
        grad_eo = (gate_value[:, None] * grad_out).astype(jnp.bfloat16)
        grad_prod = to_experts(grad_eo, target)
        grad_hidden = lax.dot_general(
            grad_prod, down_mat, (((1,), (1,)), ((), ())), preferred_element_type=jnp.float32
        )
        unused_value, gelu_pull = jax.vjp(gelu_apply, pre_act)
        grad_pre = gelu_pull(grad_hidden)[0].astype(jnp.bfloat16)
        grad_input = lax.dot_general(
            grad_pre, up_mat, (((1,), (1,)), ((), ())), preferred_element_type=jnp.float32
        )
        grad_down = lax.dot_general(
            hidden, grad_prod, (((0,), (0,)), ((), ())), preferred_element_type=jnp.float32
        )
        grad_up = lax.dot_general(
            received, grad_pre, (((0,), (0,)), ((), ())), preferred_element_type=jnp.float32
        )
        sent_up, sent_down = grad_up.astype(jnp.bfloat16), grad_down.astype(jnp.bfloat16)
        grad_input, sent_up, sent_down = lax.optimization_barrier(
            (grad_input, sent_up, sent_down)
        )
        sent_up, sent_down = send(sent_up), send(sent_down)
        grad_branch_e = from_experts(grad_input, target)
        grad_logits = gate_pull(grad_gate)[0]
        grad_branch = grad_branch_e + jnp.dot(
            grad_logits, router_mat.astype(jnp.float32).T, precision=HIGHEST
        )
        grad_router = jnp.dot(branch.astype(jnp.float32).T, grad_logits, precision=HIGHEST)
        unused_middle, norm_pull = jax.vjp(rms_apply, middle, moe_scale)
        grad_mid_norm, grad_moe_scale = norm_pull(grad_branch)
        grad_middle = grad_out + grad_mid_norm
        grad_attn = gather_rows(grad_middle.astype(jnp.bfloat16))
        grad_blend = jnp.dot(grad_attn, out_mat, preferred_element_type=jnp.float32).astype(
            jnp.bfloat16
        )
        if arrived is not None:
            grad_blend, arrived = lax.optimization_barrier((grad_blend, arrived))
        grad_packed, grad_table = split_backward(
            packed,
            rel_bias,
            allowed,
            logs,
            grad_blend.reshape(group_rows, head_count, head_dim),
            bucket_count,
        )
        flat_grad = grad_packed.reshape(group_rows, -1)
        grad_normed = sum_rows(
            lax.dot_general(
                flat_grad, qkv_mat, (((1,), (1,)), ((), ())), preferred_element_type=jnp.float32
            )
        )
        grad_out_mat = lax.dot_general(
            grad_attn,
            blended.reshape(group_rows, -1),
            (((0,), (0,)), ((), ())),
            preferred_element_type=jnp.float32,
        )
        grad_qkv = lax.dot_general(
            normed_full, flat_grad, (((0,), (0,)), ((), ())), preferred_element_type=jnp.float32
        )
        unused_resid, norm_pull_attn = jax.vjp(rms_apply, residual, attn_scale)
        grad_res_norm, grad_attn_scale = norm_pull_attn(grad_normed)
        grad_resid = (grad_middle + grad_res_norm).astype(jnp.bfloat16)
        grad_large = jnp.concatenate([grad_qkv, grad_out_mat], axis=1)
        grad_small = jnp.concatenate(
            [
                grad_attn_scale.reshape(dp_count, -1),
                grad_moe_scale.reshape(dp_count, -1),
                grad_router.reshape(dp_count, -1),
                grad_table.reshape(dp_count, -1),
            ],
            axis=1,
        )
        width = grad_large.shape[1]
        extra_rows = -(-grad_small.shape[1] // (16 * width)) * 16
        grad_small = jnp.pad(
            grad_small, ((0, 0), (0, extra_rows * width - grad_small.shape[1]))
        ).reshape(dp_count, extra_rows, width)
        grad_large = jnp.concatenate(
            [grad_large.reshape(dp_count, part, width), grad_small], axis=1
        ).astype(jnp.bfloat16)
        return (grad_resid, grad_large, sent_up, sent_down, grad_up, grad_down, arrived)

    settings = (layer_setup(0), layer_setup(1))
    layer_in = lax.dynamic_index_in_dim(inputs, section_pos, 0, keepdims=False)
    out0, stored0 = layer_forward(layer_in, settings[0], up_mats[0], down_mats[0])
    out1, stored1 = layer_forward(out0, settings[1], up_mats[1], down_mats[1])
    grad_in = lax.dynamic_index_in_dim(cotangent, section_pos, 0, keepdims=False)
    res1, large1, got_up1, got_down1, up1, down1, unused = layer_backward(
        grad_in, settings[1], stored1, up_mats[1], down_mats[1], to_second, None
    )
    res1, large1 = lax.optimization_barrier((res1, large1))
    got_large1 = to_second(large1)
    res0, large0, got_up0, got_down0, up0, down0, arrived = layer_backward(
        res1,
        settings[0],
        stored0,
        up_mats[0],
        down_mats[0],
        to_first,
        (got_up1, got_down1, got_large1),
    )
    got_up1, got_down1, got_large1 = arrived
    got_large0 = to_first(large0)

    def place(rows0, rows1):
        from_second = to_first(rows0)
        from_first = to_second(rows1)
        return jnp.where(
            first, jnp.stack([rows0, from_second]), jnp.stack([from_first, rows1])
        )[None]

    def total(grad0, grad1, from_second, from_first):
        from_second = from_second.astype(jnp.float32)
        from_first = from_first.astype(jnp.float32)
        return jnp.where(first, grad0 + from_second, grad1 + from_first)

    layer_outputs = place(out0, out1)
    input_grads = place(res0, res1)
    up_total = total(up0, up1, got_up0, got_up1)
    down_total = total(down0, down1, got_down0, got_down1)
    large_total = total(large0, large1, got_large0, got_large1).astype(jnp.bfloat16)
    large_total = lax.psum_scatter(large_total, "dp", scatter_dimension=0, tiled=True)[0]
    large_total = large_total.astype(jnp.float32)
    small_total = large_total[part:].reshape(-1)
    large_total = large_total[:part]
    router_end = (2 + experts) * part
    table_end = router_end + bucket_part * head_count
    table_total = small_total[router_end:table_end].reshape(bucket_part, head_count)
    small_total = lax.psum(small_total[:router_end], "tensor")
    return (
        layer_outputs,
        input_grads,
        small_total[:part][None],
        small_total[part : 2 * part][None],
        large_total[:, :packed_feats].reshape(part, 3, head_feats)[None],
        large_total[:, packed_feats:][None],
        table_total[None],
        small_total[2 * part : router_end].reshape(part, experts)[None],
        up_total[None, None],
        down_total[None, None],
    )


def solution(mesh):
    placed = (
        P(None, ("dp", "tensor"), None),
        P(None, ("dp", "tensor"), None),
        P(None, "dp", None),
        P("section", None, "dp", None),
        P("section", "dp"),
        P("section", "dp"),
        P("section", "dp", None, "tensor"),
        P("section", "dp", "tensor"),
        P("section", "dp", "tensor"),
        P("section", "dp", None),
        P("section", "dp", None, "tensor"),
        P("section", "dp", "tensor", None),
    )
    return jax.shard_map(
        body,
        mesh=mesh,
        in_specs=placed,
        out_specs=(
            P("section", None, ("dp", "tensor"), None),
            P("section", None, ("dp", "tensor"), None),
            P("section", "dp"),
            P("section", "dp"),
            P("section", "dp", None, "tensor"),
            P("section", "dp", "tensor"),
            P("section", "dp", "tensor"),
            P("section", "dp", None),
            P("section", "dp", None, "tensor"),
            P("section", "dp", "tensor", None),
        ),
        check_vma=False,
    )
```

profile of v0, /device:TPU:0, one launch (start us, length us, event | category | flops | bytes accessed | tf_op | source)
XLA Modules:
  0.0 1426.6 jit_solution(1388210163174007254)
XLA Ops:
  14.5 25.5 %all-reduce.4 = bf16[9408]{0:T(1024)(128)(2,1)S(1)} all-reduce(bf16[9408]{0:T(1024)(128)(2,1)S(1)} %dynamic-update-slice), channel_id=2, replica_groups=mesh['section'=2,'dp'=4,'tensor'=4] {'section','dp'}, use_global_device_ids=true, to_apply=%add.4 | all-reduce | flops 9408 | bytes 37632
  75.0 20.6 %collective-permute-done = bf16[768,768]{1,0:T(8,128)(2,1)} collective-permute-done((bf16[768,768]{1,0:T(8,128)(2,1)}, bf16[768,768]{1,0:T(8,128)(2,1)}, u32[]{:S(2)}, u32[]{:S(2)}) %collective-permute-start) | collective-permute-done | bytes 1179680 | tf_op jit(solution)/shard_map/ppermute | solution.py:50
  98.5 15.3 %all-gather.13.cloned.1.call-done = bf16[1536,768]{1,0:T(8,128)(2,1)} async-done(((bf16[192,768]{1,0:T(8,128)(2,1)}), bf16[1536,768]{1,0:T(8,128)(2,1)}) %all-gather.13.cloned.1.call-update) | async-done | bytes 2359312 | tf_op jit(solution)/shard_map/all_gather | solution.py:245
  133.9 36.9 %reduce-scatter.10.cloned.1.call-done = bf16[272,768]{1,0:T(8,128)(2,1)} async-done(((bf16[1088,768]{1,0:T(8,128)(2,1)}), bf16[272,768]{1,0:T(8,128)(2,1)}) %reduce-scatter.10.cloned.1.call-update) | async-done | bytes 417808 | tf_op jit(solution)/shard_map/reduce_scatter | solution.py:40
  179.0 32.8 %all-gather.15.cloned.1.call-done = bf16[1088,768]{1,0:T(8,128)(2,1)} async-done(((bf16[272,768]{1,0:T(8,128)(2,1)}), bf16[1088,768]{1,0:T(8,128)(2,1)}) %all-gather.15.cloned.1.call-update) | async-done | bytes 1671184 | tf_op jit(solution)/shard_map/all_gather | solution.py:36
  211.9 6.4 fusion.38
  218.3 41.7 %all_to_all.40 = bf16[4,544,768]{2,1,0:T(8,128)(2,1)S(1)} all-to-all(bf16[4,544,768]{2,1,0:T(8,128)(2,1)S(1)} %bitcast.393), channel_id=1, replica_groups=mesh['section'=2,'dp'=4,'tensor'=4] {'dp'}, dimensions={0} | all-to-all | bytes 6684672 | tf_op jit(solution)/shard_map/all_to_all | solution.py:46
  268.9 41.8 %all_to_all.41 = bf16[4,544,768]{2,1,0:T(8,128)(2,1)S(1)} all-to-all(bf16[4,544,768]{2,1,0:T(8,128)(2,1)S(1)} %bitcast.399), channel_id=1, replica_groups=mesh['section'=2,'dp'=4,'tensor'=4] {'dp'}, dimensions={0} | all-to-all | bytes 6684672 | tf_op jit(solution)/shard_map/all_to_all | solution.py:46
  310.6 5.5 fusion.52
  323.0 28.1 %reduce-scatter.12.cloned.1.call-done = bf16[272,768]{1,0:T(8,128)(2,1)} async-done(((bf16[1088,768]{1,0:T(8,128)(2,1)}), bf16[272,768]{1,0:T(8,128)(2,1)}) %reduce-scatter.12.cloned.1.call-update) | async-done | bytes 417808 | tf_op jit(solution)/shard_map/reduce_scatter | solution.py:40
  365.2 26.7 %all-gather.17.cloned.1.call-done = bf16[1088,768]{1,0:T(8,128)(2,1)} async-done(((bf16[272,768]{1,0:T(8,128)(2,1)}), bf16[1088,768]{1,0:T(8,128)(2,1)}) %all-gather.17.cloned.1.call-update) | async-done | bytes 1671184 | tf_op jit(solution)/shard_map/all_gather | solution.py:36
  410.4 35.2 %reduce-scatter.14.cloned.1.call-done = bf16[272,768]{1,0:T(8,128)(2,1)} async-done(((bf16[1088,768]{1,0:T(8,128)(2,1)}), bf16[272,768]{1,0:T(8,128)(2,1)}) %reduce-scatter.14.cloned.1.call-update) | async-done | bytes 417808 | tf_op jit(solution)/shard_map/reduce_scatter | solution.py:40
  449.5 37.3 %all-gather.19.cloned.1.call-done = bf16[1088,768]{1,0:T(8,128)(2,1)} async-done(((bf16[272,768]{1,0:T(8,128)(2,1)}), bf16[1088,768]{1,0:T(8,128)(2,1)}) %all-gather.19.cloned.1.call-update) | async-done | bytes 1671184 | tf_op jit(solution)/shard_map/all_gather | solution.py:36
  486.8 6.4 fusion.40
  493.1 41.7 %all_to_all.42 = bf16[4,544,768]{2,1,0:T(8,128)(2,1)S(1)} all-to-all(bf16[4,544,768]{2,1,0:T(8,128)(2,1)S(1)} %bitcast.395), channel_id=1, replica_groups=mesh['section'=2,'dp'=4,'tensor'=4] {'dp'}, dimensions={0} | all-to-all | bytes 6684672 | tf_op jit(solution)/shard_map/all_to_all | solution.py:46
  543.7 41.5 %all_to_all.43 = bf16[4,544,768]{2,1,0:T(8,128)(2,1)S(1)} all-to-all(bf16[4,544,768]{2,1,0:T(8,128)(2,1)S(1)} %bitcast.400), channel_id=1, replica_groups=mesh['section'=2,'dp'=4,'tensor'=4] {'dp'}, dimensions={0} | all-to-all | bytes 6684672 | tf_op jit(solution)/shard_map/all_to_all | solution.py:46
  585.2 5.5 fusion.54
  591.7 34.0 %reduce-scatter.16.cloned.1.call-done = bf16[272,768]{1,0:T(8,128)(2,1)} async-done(((bf16[1088,768]{1,0:T(8,128)(2,1)}), bf16[272,768]{1,0:T(8,128)(2,1)}) %reduce-scatter.16.cloned.1.call-update) | async-done | bytes 417808 | tf_op jit(solution)/shard_map/reduce_scatter | solution.py:40
  628.1 37.7 %all-gather.21.cloned.1.call-done = bf16[1088,768]{1,0:T(8,128)(2,1)} async-done(((bf16[272,768]{1,0:T(8,128)(2,1)}), bf16[1088,768]{1,0:T(8,128)(2,1)}) %all-gather.21.cloned.1.call-update) | async-done | bytes 1671184 | tf_op jit(solution)/shard_map/all_gather | solution.py:36
  665.8 6.4 fusion.41
  672.2 41.9 %all_to_all.44 = bf16[4,544,768]{2,1,0:T(8,128)(2,1)S(1)} all-to-all(bf16[4,544,768]{2,1,0:T(8,128)(2,1)S(1)} %bitcast.397), channel_id=1, replica_groups=mesh['section'=2,'dp'=4,'tensor'=4] {'dp'}, dimensions={0} | all-to-all | bytes 6684672 | tf_op jit(solution)/shard_map/all_to_all | solution.py:46
  714.1 8.2 fusion.29
  735.6 41.9 %all_to_all.45 = bf16[4,544,768]{2,1,0:T(8,128)(2,1)S(1)} all-to-all(bf16[4,544,768]{2,1,0:T(8,128)(2,1)S(1)} %bitcast.389), channel_id=1, replica_groups=mesh['section'=2,'dp'=4,'tensor'=4] {'dp'}, dimensions={0} | all-to-all | bytes 6684672 | tf_op jit(solution)/shard_map/all_to_all | solution.py:46
  777.5 5.5 fusion.55
  783.1 34.8 %reduce-scatter.18.cloned.1.call-done = bf16[272,768]{1,0:T(8,128)(2,1)} async-done(((bf16[1088,768]{1,0:T(8,128)(2,1)}), bf16[272,768]{1,0:T(8,128)(2,1)}) %reduce-scatter.18.cloned.1.call-update) | async-done | bytes 417808 | tf_op jit(solution)/shard_map/reduce_scatter | solution.py:40
  823.3 36.2 %all-gather.23.cloned.1.call-done = bf16[1088,768]{1,0:T(8,128)(2,1)} async-done(((bf16[272,768]{1,0:T(8,128)(2,1)}), bf16[1088,768]{1,0:T(8,128)(2,1)}) %all-gather.23.cloned.1.call-update) | async-done | bytes 1671184 | tf_op jit(solution)/shard_map/all_gather | solution.py:36
  862.7 6.8 fusion.73
  869.5 10.4 multiply_reduce_fusion.1
  880.8 11.2 fusion
  920.9 15.4 %reduce-scatter.20.cloned.1.call-done = bf16[272,768]{1,0:T(8,128)(2,1)} async-done(((bf16[1088,768]{1,0:T(8,128)(2,1)}), bf16[272,768]{1,0:T(8,128)(2,1)}) %reduce-scatter.20.cloned.1.call-update) | async-done | bytes 417808 | tf_op jit(solution)/shard_map/reduce_scatter | solution.py:40
  945.1 37.9 %all-gather.25.cloned.1.call-done = bf16[1088,768]{1,0:T(8,128)(2,1)} async-done(((bf16[272,768]{1,0:T(8,128)(2,1)}), bf16[1088,768]{1,0:T(8,128)(2,1)}) %all-gather.25.cloned.1.call-update) | async-done | bytes 1671184 | tf_op jit(solution)/shard_map/all_gather | solution.py:36
  982.9 6.4 fusion.39
  989.3 42.1 %all_to_all.46 = bf16[4,544,768]{2,1,0:T(8,128)(2,1)S(1)} all-to-all(bf16[4,544,768]{2,1,0:T(8,128)(2,1)S(1)} %bitcast.398), channel_id=1, replica_groups=mesh['section'=2,'dp'=4,'tensor'=4] {'dp'}, dimensions={0} | all-to-all | bytes 6684672 | tf_op jit(solution)/shard_map/all_to_all | solution.py:46
  1031.5 8.2 fusion.22
  1052.9 41.5 %all_to_all.47 = bf16[4,544,768]{2,1,0:T(8,128)(2,1)S(1)} all-to-all(bf16[4,544,768]{2,1,0:T(8,128)(2,1)S(1)} %bitcast.391), channel_id=1, replica_groups=mesh['section'=2,'dp'=4,'tensor'=4] {'dp'}, dimensions={0} | all-to-all | bytes 6684672 | tf_op jit(solution)/shard_map/all_to_all | solution.py:46
  1094.5 5.6 fusion.53
  1100.3 34.8 %reduce-scatter.22.cloned.1.call-done = bf16[272,768]{1,0:T(8,128)(2,1)} async-done(((bf16[1088,768]{1,0:T(8,128)(2,1)}), bf16[272,768]{1,0:T(8,128)(2,1)}) %reduce-scatter.22.cloned.1.call-update) | async-done | bytes 417808 | tf_op jit(solution)/shard_map/reduce_scatter | solution.py:40
  1149.7 28.3 %all-gather.27.cloned.1.call-done = bf16[1088,768]{1,0:T(8,128)(2,1)} async-done(((bf16[272,768]{1,0:T(8,128)(2,1)}), bf16[1088,768]{1,0:T(8,128)(2,1)}) %all-gather.27.cloned.1.call-update) | async-done | bytes 1671184 | tf_op jit(solution)/shard_map/all_gather | solution.py:36
  1180.4 17.2 %collective-permute-done.4 = bf16[768,768]{1,0:T(8,128)(2,1)} collective-permute-done((bf16[768,768]{1,0:T(8,128)(2,1)}, bf16[768,768]{1,0:T(8,128)(2,1)}, u32[]{:S(2)}, u32[]{:S(2)}) %collective-permute-start.4) | collective-permute-done | bytes 1179680 | tf_op jit(solution)/shard_map/ppermute | solution.py:54
  1197.6 24.0 %collective-permute-done.5 = bf16[768,768]{1,0:T(8,128)(2,1)} collective-permute-done((bf16[768,768]{1,0:T(8,128)(2,1)}, bf16[768,768]{1,0:T(8,128)(2,1)}, u32[]{:S(2)}, u32[]{:S(2)}) %collective-permute-start.5) | collective-permute-done | bytes 1179680 | tf_op jit(solution)/shard_map/ppermute | solution.py:54
  1222.4 6.8 fusion.70
  1229.2 10.5 multiply_reduce_fusion
  1241.1 10.6 fusion.2
  1283.5 14.6 %reduce-scatter.24.cloned.1.call-done = bf16[272,768]{1,0:T(8,128)(2,1)} async-done(((bf16[1088,768]{1,0:T(8,128)(2,1)}), bf16[272,768]{1,0:T(8,128)(2,1)}) %reduce-scatter.24.cloned.1.call-update) | async-done | bytes 417808 | tf_op jit(solution)/shard_map/reduce_scatter | solution.py:40
  1302.6 30.3 %collective-permute-done.9 = bf16[4,208,768]{2,1,0:T(8,128)(2,1)S(1)} collective-permute-done((bf16[4,208,768]{2,1,0:T(8,128)(2,1)S(1)}, bf16[4,208,768]{2,1,0:T(8,128)(2,1)S(1)}, u32[]{:S(2)}, u32[]{:S(2)}) %collective-permute-start.9) | collective-permute-done | bytes 1277984 | tf_op jit(solution)/shard_map/ppermute | solution.py:58
  1348.1 19.0 %collective-permute-done.2 = bf16[272,768]{1,0:T(8,128)(2,1)S(1)} collective-permute-done((bf16[272,768]{1,0:T(8,128)(2,1)S(1)}, bf16[272,768]{1,0:T(8,128)(2,1)S(1)}, u32[]{:S(2)}, u32[]{:S(2)}) %collective-permute-start.2) | collective-permute-done | bytes 417824 | tf_op jit(solution)/shard_map/ppermute | solution.py:58
  1375.7 16.6 %collective-permute-done.11 = bf16[768,768]{1,0:T(8,128)(2,1)S(1)} collective-permute-done((bf16[768,768]{1,0:T(8,128)(2,1)}, bf16[768,768]{1,0:T(8,128)(2,1)S(1)}, u32[]{:S(2)}, u32[]{:S(2)}) %collective-permute-start.11) | collective-permute-done | bytes 1179680 | tf_op jit(solution)/shard_map/ppermute | solution.py:58
  1401.8 10.5 psum.7
  (607 shorter events, 305.1 us)
Async XLA Ops:
  7.2 55.3 %copy-start = (s32[2,1,3]{2,1,0:T(1,128)S(1)}, s32[2,1,3]{2,1,0:T(1,128)}, u32[]{:S(2)}) copy-start(s32[2,1,3]{2,1,0:T(1,128)} %param.19) | copy-start | bytes 76
  7.2 43.3 %copy-start.129 = (s32[7]{0:T(128)S(1)}, s32[7]{0:T(128)}, u32[]{:S(2)}) copy-start(s32[7]{0:T(128)} %constant.178.clone) | copy-start | bytes 88
  7.2 91.2 %all-gather.11.cloned.1.call-start = ((), (), s32[]{:S(2)}) async-start(), calls=%async_computation.17 | async-start | bytes 2088960 | tf_op jit(solution)/shard_map/all_gather | solution.py:36
  42.8 70.9 %all-gather.13.cloned.1.call-start = ((), (), s32[]{:S(2)}) async-start(), calls=%async_computation.18 | async-start | bytes 2654208 | tf_op jit(solution)/shard_map/all_gather | solution.py:245
  42.8 29.3 %collective-permute-start.1 = (bf16[768,768]{1,0:T(8,128)(2,1)}, bf16[768,768]{1,0:T(8,128)(2,1)}, u32[]{:S(2)}, u32[]{:S(2)}) collective-permute-start(bf16[768,768]{1,0:T(8,128)(2,1)} %bitcast.404), channel_id=1, source_target_pairs={{0,16},{16,0},{1,17},{17,1},{2,18},{18,2},{3,19},{19,3},{4,20},{20... | collective-permute-start | bytes 3538952 | tf_op jit(solution)/shard_map/ppermute | solution.py:50
  43.5 52.1 %collective-permute-start = (bf16[768,768]{1,0:T(8,128)(2,1)}, bf16[768,768]{1,0:T(8,128)(2,1)}, u32[]{:S(2)}, u32[]{:S(2)}) collective-permute-start(bf16[768,768]{1,0:T(8,128)(2,1)} %bitcast.405), channel_id=1, source_target_pairs={{0,16},{16,0},{1,17},{17,1},{2,18},{18,2},{3,19},{19,3},{4,20},{20... | collective-permute-start | bytes 3538952 | tf_op jit(solution)/shard_map/ppermute | solution.py:50
  48.0 122.7 %reduce-scatter.10.cloned.1.call-start = ((), (), s32[]{:S(2)}) async-start(), calls=%async_computation.19 | async-start | bytes 2088960 | tf_op jit(solution)/shard_map/reduce_scatter | solution.py:40
  67.0 49.8 %copy-start.117 = (pred[64,64]{0,1:T(8,128)(4,1)}, pred[64,64]{0,1:T(8,128)(4,1)S(1)}, u32[]{:S(2)}) copy-start(pred[64,64]{0,1:T(8,128)(4,1)S(1)} %broadcast_compare_fusion) | copy-start | bytes 12292
  133.7 78.1 %all-gather.15.cloned.1.call-start = ((), (), s32[]{:S(2)}) async-start(), calls=%async_computation.20 | async-start | bytes 2088960 | tf_op jit(solution)/shard_map/all_gather | solution.py:36
  133.9 84.4 %copy-start.76 = (f32[768]{0:T(1024)}, f32[768]{0:T(1024)S(1)}, u32[]{:S(2)}) copy-start(f32[768]{0:T(1024)S(1)} %reshape.846) | copy-start | bytes 9220
  174.0 177.1 %reduce-scatter.12.cloned.1.call-start = ((), (), s32[]{:S(2)}) async-start(), calls=%async_computation.21 | async-start | bytes 2088960 | tf_op jit(solution)/shard_map/reduce_scatter | solution.py:40
  179.0 131.6 %copy-start.109 = (s32[1088]{0:T(1024)}, s32[1088]{0:T(1024)S(1)}, u32[]{:S(2)}) copy-start(s32[1088]{0:T(1024)S(1)} %add_add_fusion.5) | copy-start | bytes 13060
  218.2 43.5 %copy-start.52 = (bf16[768,768]{1,0:T(8,128)(2,1)S(1)}, bf16[768,768]{1,0:T(8,128)(2,1)}, u32[]{:S(2)}) copy-start(bf16[768,768]{1,0:T(8,128)(2,1)} %get-tuple-element.29) | copy-start | bytes 3538948
  316.2 75.8 %all-gather.17.cloned.1.call-start = ((), (), s32[]{:S(2)}) async-start(), calls=%async_computation.22 | async-start | bytes 2088960 | tf_op jit(solution)/shard_map/all_gather | solution.py:36
  354.0 91.6 %reduce-scatter.14.cloned.1.call-start = ((), (), s32[]{:S(2)}) async-start(), calls=%async_computation.23 | async-start | bytes 2088960 | tf_op jit(solution)/shard_map/reduce_scatter | solution.py:40
  409.8 76.9 %all-gather.19.cloned.1.call-start = ((), (), s32[]{:S(2)}) async-start(), calls=%async_computation.24 | async-start | bytes 2088960 | tf_op jit(solution)/shard_map/all_gather | solution.py:36
  448.9 176.8 %reduce-scatter.16.cloned.1.call-start = ((), (), s32[]{:S(2)}) async-start(), calls=%async_computation.25 | async-start | bytes 2088960 | tf_op jit(solution)/shard_map/reduce_scatter | solution.py:40
  493.1 43.4 %copy-start.56 = (bf16[768,768]{1,0:T(8,128)(2,1)S(1)}, bf16[768,768]{1,0:T(8,128)(2,1)}, u32[]{:S(2)}) copy-start(bf16[768,768]{1,0:T(8,128)(2,1)} %get-tuple-element.32) | copy-start | bytes 3538948
  590.8 75.0 %all-gather.21.cloned.1.call-start = ((), (), s32[]{:S(2)}) async-start(), calls=%async_computation.26 | async-start | bytes 2088960 | tf_op jit(solution)/shard_map/all_gather | solution.py:36
  591.4 226.6 %copy-start.95 = (s32[272]{0:T(512)}, s32[272]{0:T(512)S(1)}, u32[]{:S(2)}) copy-start(s32[272]{0:T(512)S(1)} %fusion.215) | copy-start | bytes 3268
  627.9 190.1 %reduce-scatter.18.cloned.1.call-start = ((), (), s32[]{:S(2)}) async-start(), calls=%async_computation.27 | async-start | bytes 2088960 | tf_op jit(solution)/shard_map/reduce_scatter | solution.py:40
  672.1 50.1 %slice-start.8 = ((s8[6684672]{0:T(1024)(128)(4,1)}), s8[4194304]{0:T(1024)(128)(4,1)S(1)}, s32[]{:S(2)}) async-start(s8[6684672]{0:T(1024)(128)(4,1)} %bitcast.436), calls=%async_computation.43 | async-start | bytes 8388608
  783.0 76.5 %all-gather.23.cloned.1.call-start = ((), (), s32[]{:S(2)}) async-start(), calls=%async_computation.28 | async-start | bytes 2088960 | tf_op jit(solution)/shard_map/all_gather | solution.py:36
  821.6 114.7 %reduce-scatter.20.cloned.1.call-start = ((), (), s32[]{:S(2)}) async-start(), calls=%async_computation.29 | async-start | bytes 2088960 | tf_op jit(solution)/shard_map/reduce_scatter | solution.py:40
  823.3 56.6 %copy-start.14 = (pred[1024,1024]{0,1:T(8,128)(4,1)}, pred[1024,1024]{0,1:T(8,128)(4,1)S(1)}, u32[]{:S(2)}) copy-start(pred[1024,1024]{0,1:T(8,128)(4,1)S(1)} %get-tuple-element.132) | copy-start | bytes 3145732
  823.3 56.6 %copy-start.16 = (pred[1024,1024]{0,1:T(8,128)(4,1)}, pred[1024,1024]{0,1:T(8,128)(4,1)S(1)}, u32[]{:S(2)}) copy-start(pred[1024,1024]{0,1:T(8,128)(4,1)S(1)} %get-tuple-element.133) | copy-start | bytes 3145732
  900.5 82.4 %all-gather.25.cloned.1.call-start = ((), (), s32[]{:S(2)}) async-start(), calls=%async_computation.30 | async-start | bytes 2088960 | tf_op jit(solution)/shard_map/all_gather | solution.py:36
  945.0 190.1 %reduce-scatter.22.cloned.1.call-start = ((), (), s32[]{:S(2)}) async-start(), calls=%async_computation.31 | async-start | bytes 2088960 | tf_op jit(solution)/shard_map/reduce_scatter | solution.py:40
  989.3 50.3 %slice-start.6 = ((s8[6684672]{0:T(1024)(128)(4,1)}), s8[4194304]{0:T(1024)(128)(4,1)S(1)}, s32[]{:S(2)}) async-start(s8[6684672]{0:T(1024)(128)(4,1)} %bitcast.434), calls=%async_computation.41 | async-start | bytes 8388608
  1100.1 77.9 %all-gather.27.cloned.1.call-start = ((), (), s32[]{:S(2)}) async-start(), calls=%async_computation.32 | async-start | bytes 2088960 | tf_op jit(solution)/shard_map/all_gather | solution.py:36
  1100.2 49.4 %copy-start.112 = (f32[3,64]{1,0:T(4,128)S(1)}, f32[3,64]{1,0:T(4,128)}, u32[]{:S(2)}) copy-start(f32[3,64]{1,0:T(4,128)} %copy-done.111) | copy-start | bytes 2308
  1100.2 49.4 %copy-start.114 = (f32[3,64]{1,0:T(4,128)S(1)}, f32[3,64]{1,0:T(4,128)}, u32[]{:S(2)}) copy-start(f32[3,64]{1,0:T(4,128)} %copy-done.113) | copy-start | bytes 2308
  1100.3 49.4 %copy-start.71 = (f32[3,1024]{1,0:T(4,128)S(1)}, f32[3,1024]{1,0:T(4,128)}, u32[]{:S(2)}) copy-start(f32[3,1024]{1,0:T(4,128)} %copy-done.70) | copy-start | bytes 36868
  1100.3 49.4 %copy-start.81 = (f32[3,1024]{1,0:T(4,128)S(1)}, f32[3,1024]{1,0:T(4,128)}, u32[]{:S(2)}) copy-start(f32[3,1024]{1,0:T(4,128)} %copy-done.80) | copy-start | bytes 36868
  1138.0 83.7 %copy-start.47 = (f32[3,64,64]{1,2,0:T(8,128)S(1)}, f32[3,64,64]{1,2,0:T(8,128)}, u32[]{:S(2)}) copy-start(f32[3,64,64]{1,2,0:T(8,128)} %copy-done.46) | copy-start | bytes 147460
  1140.1 158.0 %reduce-scatter.24.cloned.1.call-start = ((), (), s32[]{:S(2)}) async-start(), calls=%async_computation.33 | async-start | bytes 2088960 | tf_op jit(solution)/shard_map/reduce_scatter | solution.py:40
  1140.1 81.4 %collective-permute-start.6 = (bf16[4,208,768]{2,1,0:T(8,128)(2,1)}, bf16[4,208,768]{2,1,0:T(8,128)(2,1)}, u32[]{:S(2)}, u32[]{:S(2)}) collective-permute-start(bf16[4,208,768]{2,1,0:T(8,128)(2,1)} %pad_maximum_fusion.2), channel_id=1, source_target_pairs={{0,16},{1,17},{2,18},{3,19},{4,20},{5,21},{6,22},{7,23},{8,24},{9,... | collective-permute-start | bytes 3833864 | tf_op jit(solution)/shard_map/ppermute | solution.py:54
  1144.6 53.0 %collective-permute-start.4 = (bf16[768,768]{1,0:T(8,128)(2,1)}, bf16[768,768]{1,0:T(8,128)(2,1)}, u32[]{:S(2)}, u32[]{:S(2)}) collective-permute-start(bf16[768,768]{1,0:T(8,128)(2,1)} %get-tuple-element.37), channel_id=1, source_target_pairs={{0,16},{1,17},{2,18},{3,19},{4,20},{5,21},{6,22},{7,23},{8,24},{9,... | collective-permute-start | bytes 3538952 | tf_op jit(solution)/shard_map/ppermute | solution.py:54
  1146.9 74.7 %collective-permute-start.5 = (bf16[768,768]{1,0:T(8,128)(2,1)}, bf16[768,768]{1,0:T(8,128)(2,1)}, u32[]{:S(2)}, u32[]{:S(2)}) collective-permute-start(bf16[768,768]{1,0:T(8,128)(2,1)} %get-tuple-element.38), channel_id=1, source_target_pairs={{0,16},{1,17},{2,18},{3,19},{4,20},{5,21},{6,22},{7,23},{8,24},{9,... | collective-permute-start | bytes 3538952 | tf_op jit(solution)/shard_map/ppermute | solution.py:54
  1178.0 43.8 %copy-start.26 = (bf16[1088,576]{0,1:T(8,128)(2,1)S(1)}, bf16[1088,576]{0,1:T(8,128)(2,1)}, u32[]{:S(2)}) copy-start(bf16[1088,576]{0,1:T(8,128)(2,1)} %copy-done.25) | copy-start | bytes 3760132
  1260.9 140.1 %reduce-scatter.26.cloned.1.call-start = ((), (), s32[]{:S(2)}) async-start(), calls=%async_computation.34 | async-start | bytes 1597440 | tf_op jit(solution)/shard_map/reduce_scatter | solution.py:483
  1299.9 33.0 %collective-permute-start.9 = (bf16[4,208,768]{2,1,0:T(8,128)(2,1)S(1)}, bf16[4,208,768]{2,1,0:T(8,128)(2,1)S(1)}, u32[]{:S(2)}, u32[]{:S(2)}) collective-permute-start(bf16[4,208,768]{2,1,0:T(8,128)(2,1)S(1)} %pad_maximum_fusion.3), channel_id=1, source_target_pairs={{16,0},{17,1},{18,2},{19,3},{20,4},{21,5},{22,6},{23,7},{24,8},{25... | collective-permute-start | bytes 3833864 | tf_op jit(solution)/shard_map/ppermute | solution.py:58
  1301.3 67.9 %collective-permute-start.10 = (bf16[768,768]{1,0:T(8,128)(2,1)}, bf16[768,768]{1,0:T(8,128)(2,1)}, u32[]{:S(2)}, u32[]{:S(2)}) collective-permute-start(bf16[768,768]{1,0:T(8,128)(2,1)} %get-tuple-element.42), channel_id=1, source_target_pairs={{16,0},{17,1},{18,2},{19,3},{20,4},{21,5},{22,6},{23,7},{24,8},{25... | collective-permute-start | bytes 3538952 | tf_op jit(solution)/shard_map/ppermute | solution.py:58
  1336.1 31.0 %collective-permute-start.2 = (bf16[272,768]{1,0:T(8,128)(2,1)S(1)}, bf16[272,768]{1,0:T(8,128)(2,1)S(1)}, u32[]{:S(2)}, u32[]{:S(2)}) collective-permute-start(bf16[272,768]{1,0:T(8,128)(2,1)S(1)} %get-tuple-element.101), channel_id=1, source_target_pairs={{16,0},{17,1},{18,2},{19,3},{20,4},{21,5},{22,6},{23,7},{24,8},{25... | collective-permute-start | bytes 1253384 | tf_op jit(solution)/shard_map/ppermute | solution.py:58
  1337.5 29.6 %collective-permute-start.3 = (bf16[272,768]{1,0:T(8,128)(2,1)}, bf16[272,768]{1,0:T(8,128)(2,1)S(1)}, u32[]{:S(2)}, u32[]{:S(2)}) collective-permute-start(bf16[272,768]{1,0:T(8,128)(2,1)} %get-tuple-element.111), channel_id=1, source_target_pairs={{0,16},{1,17},{2,18},{3,19},{4,20},{5,21},{6,22},{7,23},{8,24},{9,... | collective-permute-start | bytes 1253384 | tf_op jit(solution)/shard_map/ppermute | solution.py:54
  1342.1 50.3 %collective-permute-start.11 = (bf16[768,768]{1,0:T(8,128)(2,1)}, bf16[768,768]{1,0:T(8,128)(2,1)S(1)}, u32[]{:S(2)}, u32[]{:S(2)}) collective-permute-start(bf16[768,768]{1,0:T(8,128)(2,1)} %get-tuple-element.44), channel_id=1, source_target_pairs={{16,0},{17,1},{18,2},{19,3},{20,4},{21,5},{22,6},{23,7},{24,8},{25... | collective-permute-start | bytes 3538952 | tf_op jit(solution)/shard_map/ppermute | solution.py:58
  1343.4 52.1 %collective-permute-start.8 = (bf16[272,768]{1,0:T(8,128)(2,1)}, bf16[272,768]{1,0:T(8,128)(2,1)S(1)}, u32[]{:S(2)}, u32[]{:S(2)}) collective-permute-start(bf16[272,768]{1,0:T(8,128)(2,1)} %copy-done.12), channel_id=1, source_target_pairs={{0,16},{1,17},{2,18},{3,19},{4,20},{5,21},{6,22},{7,23},{8,24},{9,... | collective-permute-start | bytes 1253384 | tf_op jit(solution)/shard_map/ppermute | solution.py:54
  1374.3 25.7 %collective-permute-start.7 = (bf16[272,768]{1,0:T(8,128)(2,1)S(1)}, bf16[272,768]{1,0:T(8,128)(2,1)S(1)}, u32[]{:S(2)}, u32[]{:S(2)}) collective-permute-start(bf16[272,768]{1,0:T(8,128)(2,1)S(1)} %fusion.111), channel_id=1, source_target_pairs={{16,0},{17,1},{18,2},{19,3},{20,4},{21,5},{22,6},{23,7},{24,8},{25... | collective-permute-start | bytes 1253384 | tf_op jit(solution)/shard_map/ppermute | solution.py:58
  (124 other events, 1504.4 us)
Sparse Core Ops, SparseCore 0:
  42.9 38.0 all-gather.10
  83.5 30.1 all-gather.12
  133.9 36.8 reduce-scatter.9
  174.1 37.7 all-gather.14
  316.3 34.7 reduce-scatter.11
  354.2 37.7 all-gather.16
  410.0 35.6 reduce-scatter.13
  449.0 37.7 all-gather.18
  590.9 34.7 reduce-scatter.15
  628.0 37.7 all-gather.20
  783.2 34.7 reduce-scatter.17
  821.7 37.7 all-gather.22
  900.6 35.6 reduce-scatter.19
  945.1 37.7 all-gather.24
  1100.3 34.7 reduce-scatter.21
  1140.2 37.7 all-gather.26
  1261.0 37.0 reduce-scatter.23
  1336.2 24.4 reduce-scatter.25
where the time goes:
time: 1440 us; the launch traced here: 1430 us
  waiting for transfers between devices  624 us (43%)
  blocking collectives  375 us (26%)
  matrix products  204 us (14%)
  other arithmetic  115 us (8%)
  local copies, waits for them, and re-layouts  62.5 us (4%)
  starting transfers between devices  29.4 us (2%)
  between operations  17.4 us (1%)
    all_to_all x8, blocking collectives, exchange(): return lax.all_to_all(piece, 'dp', split_axis=0, concat_axis=0, tiled=True)  334 us
    all_gather x8, waiting for transfers between devices, gather_rows(): return lax.all_gather(piece, 'tensor', axis=0, tiled=True)  237 us
    reduce_scatter x8, waiting for transfers between devices, sum_rows(): lax.psum_scatter(piece.astype(jnp.bfloat16), 'tensor', scatter_dimension=...  234 us
    ppermute x5, waiting for transfers between devices, to_first(): return lax.ppermute(piece, 'section', [(1, 0)])  70.4 us
    ppermute x5, waiting for transfers between devices, to_second(): return lax.ppermute(piece, 'section', [(0, 1)])  41.2 us
    unnamed x312, local copies, waits for them, and re-layouts  38.2 us
  transfers between devices with their start and end apart: 30, of which 24 were waited for; matrix products, arithmetic and copies ran while one was open for 7% of the time, Pallas kernels for 0%

commit v1 on v0

--- a/solution.py
+++ b/solution.py
@@ -287,12 +287,14 @@
         ).astype(jnp.bfloat16)
         return exchange(outgoing.reshape(experts, capacity, model_dim)).reshape(-1, model_dim)
 
-    def from_experts(produced, target):
+    def from_experts(produced, target, beside=()):
         produced = produced.astype(jnp.bfloat16).reshape(experts, capacity, model_dim)
-        returned = exchange(produced).reshape(slots, model_dim)
+        returned = exchange(produced)
+        returned, beside = lax.optimization_barrier((returned, beside))
+        returned = returned.reshape(slots, model_dim)
         chosen = (target[:, None] == places_all[None, :]).astype(jnp.bfloat16)
         own = jnp.dot(chosen, returned, preferred_element_type=jnp.float32)
-        return sum_rows(own)
+        return sum_rows(own), beside
 
     def layer_forward(layer_in, setting, up_mat, down_mat):
         target, own_choose, attn_scale, moe_scale, router_mat, qkv_mat, out_mat, rel_bias = setting
@@ -301,7 +303,6 @@
         normed_full = gather_rows(normed)
         packed = jnp.dot(normed_full, qkv_mat, preferred_element_type=jnp.float32)
         packed = packed.astype(jnp.bfloat16).reshape(group_rows, 3, head_count, head_dim)
-        packed, up_mat, down_mat = lax.optimization_barrier((packed, up_mat, down_mat))
         blended, logs = split_forward(packed, rel_bias, allowed)
         attn_full = lax.dot_general(
             blended.reshape(group_rows, -1),
@@ -313,10 +314,11 @@
         branch = rms_apply(middle, moe_scale).astype(jnp.bfloat16)
         logits = jnp.dot(branch, router_mat, preferred_element_type=jnp.float32)
         received = to_experts(branch, target)
+        received, up_mat, down_mat = lax.optimization_barrier((received, up_mat, down_mat))
         pre_act = jnp.dot(received, up_mat, preferred_element_type=jnp.float32)
         hidden = gelu_apply(pre_act).astype(jnp.bfloat16)
         produced = jnp.dot(hidden, down_mat, preferred_element_type=jnp.float32)
-        own_out = from_experts(produced, target).astype(jnp.bfloat16)
+        own_out = from_experts(produced, target)[0].astype(jnp.bfloat16)
         chances = jax.nn.softmax(logits, axis=-1)
         gate_value = jnp.sum(chances * own_choose, axis=-1)
         result = (middle + gate_value[:, None] * own_out.astype(jnp.float32)).astype(jnp.bfloat16)
@@ -336,7 +338,7 @@
         )
         return (result, stored)
 
-    def layer_backward(grad_in, setting, stored, up_mat, down_mat, send, arrived):
+    def layer_backward(grad_in, setting, stored, up_mat, down_mat, send):
         target, own_choose, attn_scale, moe_scale, router_mat, qkv_mat, out_mat, rel_bias = setting
         (
             residual,
@@ -380,7 +382,9 @@
             (grad_input, sent_up, sent_down)
         )
         sent_up, sent_down = send(sent_up), send(sent_down)
-        grad_branch_e = from_experts(grad_input, target)
+        grad_branch_e, (sent_up, sent_down) = from_experts(
+            grad_input, target, (sent_up, sent_down)
+        )
         grad_logits = gate_pull(grad_gate)[0]
         grad_branch = grad_branch_e + jnp.dot(
             grad_logits, router_mat.astype(jnp.float32).T, precision=HIGHEST
@@ -393,8 +397,6 @@
         grad_blend = jnp.dot(grad_attn, out_mat, preferred_element_type=jnp.float32).astype(
             jnp.bfloat16
         )
-        if arrived is not None:
-            grad_blend, arrived = lax.optimization_barrier((grad_blend, arrived))
         grad_packed, grad_table = split_backward(
             packed,
             rel_bias,
@@ -439,28 +441,22 @@
         grad_large = jnp.concatenate(
             [grad_large.reshape(dp_count, part, width), grad_small], axis=1
         ).astype(jnp.bfloat16)
-        return (grad_resid, grad_large, sent_up, sent_down, grad_up, grad_down, arrived)
+        return (grad_resid, grad_large, sent_up, sent_down, grad_up, grad_down)
 
     settings = (layer_setup(0), layer_setup(1))
     layer_in = lax.dynamic_index_in_dim(inputs, section_pos, 0, keepdims=False)
     out0, stored0 = layer_forward(layer_in, settings[0], up_mats[0], down_mats[0])
     out1, stored1 = layer_forward(out0, settings[1], up_mats[1], down_mats[1])
     grad_in = lax.dynamic_index_in_dim(cotangent, section_pos, 0, keepdims=False)
-    res1, large1, got_up1, got_down1, up1, down1, unused = layer_backward(
-        grad_in, settings[1], stored1, up_mats[1], down_mats[1], to_second, None
-    )
-    res1, large1 = lax.optimization_barrier((res1, large1))
+    res1, large1, got_up1, got_down1, up1, down1 = layer_backward(
+        grad_in, settings[1], stored1, up_mats[1], down_mats[1], to_second
+    )
+    large1 = lax.psum_scatter(large1, "dp", scatter_dimension=0, tiled=True)
     got_large1 = to_second(large1)
-    res0, large0, got_up0, got_down0, up0, down0, arrived = layer_backward(
-        res1,
-        settings[0],
-        stored0,
-        up_mats[0],
-        down_mats[0],
-        to_first,
-        (got_up1, got_down1, got_large1),
-    )
-    got_up1, got_down1, got_large1 = arrived
+    res0, large0, got_up0, got_down0, up0, down0 = layer_backward(
+        res1, settings[0], stored0, up_mats[0], down_mats[0], to_first
+    )
+    large0 = lax.psum_scatter(large0, "dp", scatter_dimension=0, tiled=True)
     got_large0 = to_first(large0)
 
     def place(rows0, rows1):
@@ -473,15 +469,17 @@
     def total(grad0, grad1, from_second, from_first):
         from_second = from_second.astype(jnp.float32)
         from_first = from_first.astype(jnp.float32)
-        return jnp.where(first, grad0 + from_second, grad1 + from_first)
+        return jnp.where(
+            first,
+            grad0.astype(jnp.float32) + from_second,
+            grad1.astype(jnp.float32) + from_first,
+        )
 
     layer_outputs = place(out0, out1)
     input_grads = place(res0, res1)
     up_total = total(up0, up1, got_up0, got_up1)
     down_total = total(down0, down1, got_down0, got_down1)
-    large_total = total(large0, large1, got_large0, got_large1).astype(jnp.bfloat16)
-    large_total = lax.psum_scatter(large_total, "dp", scatter_dimension=0, tiled=True)[0]
-    large_total = large_total.astype(jnp.float32)
+    large_total = total(large0, large1, got_large0, got_large1)[0]
     small_total = large_total[part:].reshape(-1)
     large_total = large_total[:part]
     router_end = (2 + experts) * part

time: 1440 us -> 1430 us (level)
  blocking collectives: 375 us -> 251 us
  waiting for transfers between devices: 624 us -> 711 us
  matrix products: 204 us -> 222 us
    all_to_all x8 -> x5, blocking collectives: 334 us -> 209 us  [exchange(): return lax.all_to_all(piece, 'dp', split_axis=0, concat_axis=0, tiled=True)]
    ppermute x2, waiting for transfers between devices: 25.8 us -> 48.5 us  [swap_section(): return lax.ppermute(piece, 'section', [(0, 1), (1, 0)])]
    all_gather x8, waiting for transfers between devices: 237 us -> 259 us  [gather_rows(): return lax.all_gather(piece, 'tensor', axis=0, tiled=True)]
    reduce_scatter x1 -> x2, waiting for transfers between devices: 0.01 us -> 19 us  [the longest x1 19 us: body(): large0 = lax.psum_scatter(large0, 'dp', scatter_dimension=0, tiled=True)]
    all_gather x1, waiting for transfers between devices: 15.3 us -> 30.4 us  [body(): larges = lax.all_gather(large, ('section', 'dp'), axis=0, tiled=True)]
    unnamed x312 -> x302, local copies, waits for them, and re-layouts: 38.2 us -> 33.7 us
  transfers between devices with their start and end apart: 30 -> 34, of which waited for: 24 -> 26; matrix products, arithmetic and copies ran while one was open for 7% -> 8% of each run, Pallas kernels for 0% -> 0%
where the time goes in v1:
time: 1430 us; the launch traced here: 1420 us
  waiting for transfers between devices  711 us (50%)
  blocking collectives  251 us (18%)
  matrix products  222 us (16%)
  other arithmetic  118 us (8%)
  local copies, waits for them, and re-layouts  59.7 us (4%)
  starting transfers between devices  41.9 us (3%)
  between operations  17.5 us (1%)
    all_gather x8, waiting for transfers between devices, gather_rows(): return lax.all_gather(piece, 'tensor', axis=0, tiled=True)  259 us
    reduce_scatter x8, waiting for transfers between devices, sum_rows(): lax.psum_scatter(piece.astype(jnp.bfloat16), 'tensor', scatter_dimension=...  241 us
    all_to_all x5, blocking collectives, exchange(): return lax.all_to_all(piece, 'dp', split_axis=0, concat_axis=0, tiled=True)  209 us
    ppermute x5, waiting for transfers between devices, to_first(): return lax.ppermute(piece, 'section', [(1, 0)])  60.7 us
    ppermute x5, waiting for transfers between devices, to_second(): return lax.ppermute(piece, 'section', [(0, 1)])  51.6 us
    ppermute x2, waiting for transfers between devices, swap_section(): return lax.ppermute(piece, 'section', [(0, 1), (1, 0)])  48.5 us
    unnamed x302, local copies, waits for them, and re-layouts  33.7 us
    all_gather x1, waiting for transfers between devices, body(): larges = lax.all_gather(large, ('section', 'dp'), axis=0, tiled=True)  30.4 us
  transfers between devices with their start and end apart: 34, of which 26 were waited for; matrix products, arithmetic and copies ran while one was open for 8% of the time, Pallas kernels for 0%

profile of v1, /device:TPU:0, one launch (start us, length us, event | category | flops | bytes accessed | tf_op | source)
XLA Modules:
  0.0 1420.3 jit_solution(15266701614546302053)
XLA Ops:
  14.5 25.5 %all-reduce.4 = bf16[9408]{0:T(1024)(128)(2,1)S(1)} all-reduce(bf16[9408]{0:T(1024)(128)(2,1)S(1)} %dynamic-update-slice), channel_id=2, replica_groups=mesh['section'=2,'dp'=4,'tensor'=4] {'section','dp'}, use_global_device_ids=true, to_apply=%add.4 | all-reduce | flops 9408 | bytes 37632
  64.7 16.3 %all-gather.11.cloned.1.call-done = bf16[1088,768]{1,0:T(8,128)(2,1)} async-done(((bf16[272,768]{1,0:T(8,128)(2,1)}), bf16[1088,768]{1,0:T(8,128)(2,1)}) %all-gather.11.cloned.1.call-update) | async-done | bytes 1671184 | tf_op jit(solution)/shard_map/all_gather | solution.py:36
  81.0 30.4 %all-gather.13.cloned.1.call-done = bf16[1536,768]{1,0:T(8,128)(2,1)} async-done(((bf16[192,768]{1,0:T(8,128)(2,1)}), bf16[1536,768]{1,0:T(8,128)(2,1)}) %all-gather.13.cloned.1.call-update) | async-done | bytes 2359312 | tf_op jit(solution)/shard_map/all_gather | solution.py:245
  131.0 36.9 %reduce-scatter.11.cloned.1.call-done = bf16[272,768]{1,0:T(8,128)(2,1)} async-done(((bf16[1088,768]{1,0:T(8,128)(2,1)}), bf16[272,768]{1,0:T(8,128)(2,1)}) %reduce-scatter.11.cloned.1.call-update) | async-done | bytes 417808 | tf_op jit(solution)/shard_map/reduce_scatter | solution.py:40
  176.0 32.9 %all-gather.15.cloned.1.call-done = bf16[1088,768]{1,0:T(8,128)(2,1)} async-done(((bf16[272,768]{1,0:T(8,128)(2,1)}), bf16[1088,768]{1,0:T(8,128)(2,1)}) %all-gather.15.cloned.1.call-update) | async-done | bytes 1671184 | tf_op jit(solution)/shard_map/all_gather | solution.py:36
  208.9 7.5 fusion.38
  223.3 27.1 %collective-permute-done.1 = bf16[768,768]{1,0:T(8,128)(2,1)} collective-permute-done((bf16[768,768]{1,0:T(8,128)(2,1)}, bf16[768,768]{1,0:T(8,128)(2,1)}, u32[]{:S(2)}, u32[]{:S(2)}) %collective-permute-start.1) | collective-permute-done | bytes 1179680 | tf_op jit(solution)/shard_map/ppermute | solution.py:50
  253.6 21.4 %collective-permute-done = bf16[768,768]{1,0:T(8,128)(2,1)} collective-permute-done((bf16[768,768]{1,0:T(8,128)(2,1)}, bf16[768,768]{1,0:T(8,128)(2,1)}, u32[]{:S(2)}, u32[]{:S(2)}) %collective-permute-start) | collective-permute-done | bytes 1179680 | tf_op jit(solution)/shard_map/ppermute | solution.py:50
  287.7 42.2 %all_to_all.40 = bf16[4,544,768]{2,1,0:T(8,128)(2,1)S(1)} all-to-all(bf16[4,544,768]{2,1,0:T(8,128)(2,1)S(1)} %bitcast.385), channel_id=1, replica_groups=mesh['section'=2,'dp'=4,'tensor'=4] {'dp'}, dimensions={0} | all-to-all | bytes 6684672 | tf_op jit(solution)/shard_map/all_to_all | solution.py:46
  329.9 5.5 fusion.52
  342.3 28.0 %reduce-scatter.13.cloned.1.call-done = bf16[272,768]{1,0:T(8,128)(2,1)} async-done(((bf16[1088,768]{1,0:T(8,128)(2,1)}), bf16[272,768]{1,0:T(8,128)(2,1)}) %reduce-scatter.13.cloned.1.call-update) | async-done | bytes 417808 | tf_op jit(solution)/shard_map/reduce_scatter | solution.py:40
  384.3 26.9 %all-gather.17.cloned.1.call-done = bf16[1088,768]{1,0:T(8,128)(2,1)} async-done(((bf16[272,768]{1,0:T(8,128)(2,1)}), bf16[1088,768]{1,0:T(8,128)(2,1)}) %all-gather.17.cloned.1.call-update) | async-done | bytes 1671184 | tf_op jit(solution)/shard_map/all_gather | solution.py:36
  430.6 35.5 %reduce-scatter.15.cloned.1.call-done = bf16[272,768]{1,0:T(8,128)(2,1)} async-done(((bf16[1088,768]{1,0:T(8,128)(2,1)}), bf16[272,768]{1,0:T(8,128)(2,1)}) %reduce-scatter.15.cloned.1.call-update) | async-done | bytes 417808 | tf_op jit(solution)/shard_map/reduce_scatter | solution.py:40
  469.9 37.2 %all-gather.19.cloned.1.call-done = bf16[1088,768]{1,0:T(8,128)(2,1)} async-done(((bf16[272,768]{1,0:T(8,128)(2,1)}), bf16[1088,768]{1,0:T(8,128)(2,1)}) %all-gather.19.cloned.1.call-update) | async-done | bytes 1671184 | tf_op jit(solution)/shard_map/all_gather | solution.py:36
  507.2 6.4 fusion.40
  513.5 41.7 %all_to_all.41 = bf16[4,544,768]{2,1,0:T(8,128)(2,1)S(1)} all-to-all(bf16[4,544,768]{2,1,0:T(8,128)(2,1)S(1)} %bitcast.381), channel_id=1, replica_groups=mesh['section'=2,'dp'=4,'tensor'=4] {'dp'}, dimensions={0} | all-to-all | bytes 6684672 | tf_op jit(solution)/shard_map/all_to_all | solution.py:46
  564.1 41.5 %all_to_all.42 = bf16[4,544,768]{2,1,0:T(8,128)(2,1)S(1)} all-to-all(bf16[4,544,768]{2,1,0:T(8,128)(2,1)S(1)} %bitcast.386), channel_id=1, replica_groups=mesh['section'=2,'dp'=4,'tensor'=4] {'dp'}, dimensions={0} | all-to-all | bytes 6684672 | tf_op jit(solution)/shard_map/all_to_all | solution.py:46
  605.6 5.5 fusion.54
  612.5 33.6 %reduce-scatter.17.cloned.1.call-done = bf16[272,768]{1,0:T(8,128)(2,1)} async-done(((bf16[1088,768]{1,0:T(8,128)(2,1)}), bf16[272,768]{1,0:T(8,128)(2,1)}) %reduce-scatter.17.cloned.1.call-update) | async-done | bytes 417808 | tf_op jit(solution)/shard_map/reduce_scatter | solution.py:40
  648.3 37.9 %all-gather.21.cloned.1.call-done = bf16[1088,768]{1,0:T(8,128)(2,1)} async-done(((bf16[272,768]{1,0:T(8,128)(2,1)}), bf16[1088,768]{1,0:T(8,128)(2,1)}) %all-gather.21.cloned.1.call-update) | async-done | bytes 1671184 | tf_op jit(solution)/shard_map/all_gather | solution.py:36
  686.2 6.4 fusion.41
  692.6 41.9 %all_to_all.43 = bf16[4,544,768]{2,1,0:T(8,128)(2,1)S(1)} all-to-all(bf16[4,544,768]{2,1,0:T(8,128)(2,1)S(1)} %bitcast.383), channel_id=1, replica_groups=mesh['section'=2,'dp'=4,'tensor'=4] {'dp'}, dimensions={0} | all-to-all | bytes 6684672 | tf_op jit(solution)/shard_map/all_to_all | solution.py:46
  734.5 8.2 fusion.29
  768.0 24.0 %collective-permute-done.4 = bf16[768,768]{1,0:T(8,128)(2,1)S(1)} collective-permute-done((bf16[768,768]{1,0:T(8,128)(2,1)}, bf16[768,768]{1,0:T(8,128)(2,1)S(1)}, u32[]{:S(2)}, u32[]{:S(2)}) %collective-permute-start.4) | collective-permute-done | bytes 1179680 | tf_op jit(solution)/shard_map/ppermute | solution.py:54
  792.0 24.8 %collective-permute-done.5 = bf16[768,768]{1,0:T(8,128)(2,1)} collective-permute-done((bf16[768,768]{1,0:T(8,128)(2,1)}, bf16[768,768]{1,0:T(8,128)(2,1)}, u32[]{:S(2)}, u32[]{:S(2)}) %collective-permute-start.5) | collective-permute-done | bytes 1179680 | tf_op jit(solution)/shard_map/ppermute | solution.py:54
  816.8 7.6 fusion.55
  824.5 36.9 %reduce-scatter.19.cloned.1.call-done = bf16[272,768]{1,0:T(8,128)(2,1)} async-done(((bf16[1088,768]{1,0:T(8,128)(2,1)}), bf16[272,768]{1,0:T(8,128)(2,1)}) %reduce-scatter.19.cloned.1.call-update) | async-done | bytes 417808 | tf_op jit(solution)/shard_map/reduce_scatter | solution.py:40
  866.1 37.8 %all-gather.23.cloned.1.call-done = bf16[1088,768]{1,0:T(8,128)(2,1)} async-done(((bf16[272,768]{1,0:T(8,128)(2,1)}), bf16[1088,768]{1,0:T(8,128)(2,1)}) %all-gather.23.cloned.1.call-update) | async-done | bytes 1671184 | tf_op jit(solution)/shard_map/all_gather | solution.py:36
  908.6 6.8 fusion.73
  915.4 10.4 multiply_reduce_fusion.1
  926.7 6.1 multiply_convert_fusion.1
  942.5 35.3 %reduce-scatter.21.cloned.1.call-done = bf16[272,768]{1,0:T(8,128)(2,1)} async-done(((bf16[1088,768]{1,0:T(8,128)(2,1)}), bf16[272,768]{1,0:T(8,128)(2,1)}) %reduce-scatter.21.cloned.1.call-update) | async-done | bytes 417808 | tf_op jit(solution)/shard_map/reduce_scatter | solution.py:40
  983.5 37.9 %all-gather.25.cloned.1.call-done = bf16[1088,768]{1,0:T(8,128)(2,1)} async-done(((bf16[272,768]{1,0:T(8,128)(2,1)}), bf16[1088,768]{1,0:T(8,128)(2,1)}) %all-gather.25.cloned.1.call-update) | async-done | bytes 1671184 | tf_op jit(solution)/shard_map/all_gather | solution.py:36
  1021.4 6.4 fusion.39
  1027.7 41.9 %all_to_all.44 = bf16[4,544,768]{2,1,0:T(8,128)(2,1)S(1)} all-to-all(bf16[4,544,768]{2,1,0:T(8,128)(2,1)S(1)} %bitcast.384), channel_id=1, replica_groups=mesh['section'=2,'dp'=4,'tensor'=4] {'dp'}, dimensions={0} | all-to-all | bytes 6684672 | tf_op jit(solution)/shard_map/all_to_all | solution.py:46
  1069.7 8.1 fusion.22
  1082.7 6.5 fusion.197
  1100.9 28.0 %collective-permute-done.6 = bf16[768,768]{1,0:T(8,128)(2,1)} collective-permute-done((bf16[768,768]{1,0:T(8,128)(2,1)S(1)}, bf16[768,768]{1,0:T(8,128)(2,1)}, u32[]{:S(2)}, u32[]{:S(2)}) %collective-permute-start.6) | collective-permute-done | bytes 1179680 | tf_op jit(solution)/shard_map/ppermute | solution.py:58
  1128.9 24.8 %collective-permute-done.7 = bf16[768,768]{1,0:T(8,128)(2,1)} collective-permute-done((bf16[768,768]{1,0:T(8,128)(2,1)S(1)}, bf16[768,768]{1,0:T(8,128)(2,1)}, u32[]{:S(2)}, u32[]{:S(2)}) %collective-permute-start.7) | collective-permute-done | bytes 1179680 | tf_op jit(solution)/shard_map/ppermute | solution.py:58
  1153.8 7.6 fusion.53
  1161.6 34.9 %reduce-scatter.23.cloned.1.call-done = bf16[272,768]{1,0:T(8,128)(2,1)} async-done(((bf16[1088,768]{1,0:T(8,128)(2,1)}), bf16[272,768]{1,0:T(8,128)(2,1)}) %reduce-scatter.23.cloned.1.call-update) | async-done | bytes 417808 | tf_op jit(solution)/shard_map/reduce_scatter | solution.py:40
  1205.6 32.5 %all-gather.27.cloned.1.call-done = bf16[1088,768]{1,0:T(8,128)(2,1)} async-done(((bf16[272,768]{1,0:T(8,128)(2,1)}), bf16[1088,768]{1,0:T(8,128)(2,1)}) %all-gather.27.cloned.1.call-update) | async-done | bytes 1671184 | tf_op jit(solution)/shard_map/all_gather | solution.py:36
  1241.2 7.6 fusion.70
  1248.8 10.5 multiply_reduce_fusion
  1260.8 18.4 %fusion.2 = (f32[3]{0:T(128)}, f32[3]{0:T(128)}, f32[3]{0:T(128)}, f32[3]{0:T(128)}, bf16[3,1024,1024]{1,2,0:T(8,128)(2,1)}) fusion(bf16[3,1024,1024]{1,2,0:T(8,128)(2,1)S(1)} %bitcast.348, pred[1024,1024]{0,1:T(8,128)(4,1)} %get-tuple-element.135, pred[1024,1024]{0,1:T(8,128)(4,1)} %get-tuple-element.134, f32[3,1024,1024]{1,2,0:T(8,128)} %get-tuple-element.169, ...), kind=kLoop, calls=%fused_computation.10 | loop fusion | flops 44040176 | bytes 39870512 | tf_op jit(solution)/shard_map/reduce_sum | solution.py:124
  1312.2 7.2 select_reduce_fusion.1
  1364.7 19.0 %reduce-scatter.27.cloned.1.call-done = bf16[1,208,768]{2,1,0:T(8,128)(2,1)} async-done(((bf16[4,208,768]{2,1,0:T(8,128)(2,1)}), bf16[1,208,768]{2,1,0:T(8,128)(2,1)}) %reduce-scatter.27.cloned.1.call-update) | async-done | bytes 319504 | tf_op jit(solution)/shard_map/reduce_scatter | solution.py:459
  1395.3 11.8 psum.7
  (606 shorter events, 313.6 us)
Async XLA Ops:
  7.2 45.6 %copy-start = (s32[2,1,3]{2,1,0:T(1,128)S(1)}, s32[2,1,3]{2,1,0:T(1,128)}, u32[]{:S(2)}) copy-start(s32[2,1,3]{2,1,0:T(1,128)} %param.19) | copy-start | bytes 76
  7.2 73.8 %all-gather.11.cloned.1.call-start = ((), (), s32[]{:S(2)}) async-start(), calls=%async_computation.18 | async-start | bytes 2088960 | tf_op jit(solution)/shard_map/all_gather | solution.py:36
  42.8 68.6 %all-gather.13.cloned.1.call-start = ((), (), s32[]{:S(2)}) async-start(), calls=%async_computation.19 | async-start | bytes 2654208 | tf_op jit(solution)/shard_map/all_gather | solution.py:245
  45.9 121.9 %reduce-scatter.11.cloned.1.call-start = ((), (), s32[]{:S(2)}) async-start(), calls=%async_computation.20 | async-start | bytes 2088960 | tf_op jit(solution)/shard_map/reduce_scatter | solution.py:40
  64.7 49.9 %copy-start.109 = (pred[64,64]{0,1:T(8,128)(4,1)}, pred[64,64]{0,1:T(8,128)(4,1)S(1)}, u32[]{:S(2)}) copy-start(pred[64,64]{0,1:T(8,128)(4,1)S(1)} %broadcast_compare_fusion) | copy-start | bytes 12292
  130.8 78.1 %all-gather.15.cloned.1.call-start = ((), (), s32[]{:S(2)}) async-start(), calls=%async_computation.21 | async-start | bytes 2088960 | tf_op jit(solution)/shard_map/all_gather | solution.py:36
  131.0 85.5 %copy-start.64 = (f32[768]{0:T(1024)}, f32[768]{0:T(1024)S(1)}, u32[]{:S(2)}) copy-start(f32[768]{0:T(1024)S(1)} %reshape.843) | copy-start | bytes 9220
  176.0 153.9 %copy-start.103 = (s32[1088]{0:T(1024)}, s32[1088]{0:T(1024)S(1)}, u32[]{:S(2)}) copy-start(s32[1088]{0:T(1024)S(1)} %add_add_fusion.5) | copy-start | bytes 13060
  216.5 61.8 %all-to-all-start = ((bf16[4,544,768]{2,1,0:T(8,128)(2,1)}), bf16[4,544,768]{2,1,0:T(8,128)(2,1)}, u32[]{:S(2)}, u32[]{:S(2)}) async-start(bf16[4,544,768]{2,1,0:T(8,128)(2,1)} %bitcast.373), calls=%async_computation.1 | async-start | bytes 6684672 | tf_op jit(solution)/shard_map/all_to_all | solution.py:46
  221.2 149.2 %reduce-scatter.13.cloned.1.call-start = ((), (), s32[]{:S(2)}) async-start(), calls=%async_computation.22 | async-start | bytes 2088960 | tf_op jit(solution)/shard_map/reduce_scatter | solution.py:40
  221.2 29.2 %collective-permute-start.1 = (bf16[768,768]{1,0:T(8,128)(2,1)}, bf16[768,768]{1,0:T(8,128)(2,1)}, u32[]{:S(2)}, u32[]{:S(2)}) collective-permute-start(bf16[768,768]{1,0:T(8,128)(2,1)} %bitcast.389), channel_id=1, source_target_pairs={{0,16},{16,0},{1,17},{17,1},{2,18},{18,2},{3,19},{19,3},{4,20},{20... | collective-permute-start | bytes 3538952 | tf_op jit(solution)/shard_map/ppermute | solution.py:50
  222.7 52.3 %collective-permute-start = (bf16[768,768]{1,0:T(8,128)(2,1)}, bf16[768,768]{1,0:T(8,128)(2,1)}, u32[]{:S(2)}, u32[]{:S(2)}) collective-permute-start(bf16[768,768]{1,0:T(8,128)(2,1)} %bitcast.390), channel_id=1, source_target_pairs={{0,16},{16,0},{1,17},{17,1},{2,18},{18,2},{3,19},{19,3},{4,20},{20... | collective-permute-start | bytes 3538952 | tf_op jit(solution)/shard_map/ppermute | solution.py:50
  335.5 75.7 %all-gather.17.cloned.1.call-start = ((), (), s32[]{:S(2)}) async-start(), calls=%async_computation.23 | async-start | bytes 2088960 | tf_op jit(solution)/shard_map/all_gather | solution.py:36
  373.3 92.8 %reduce-scatter.15.cloned.1.call-start = ((), (), s32[]{:S(2)}) async-start(), calls=%async_computation.24 | async-start | bytes 2088960 | tf_op jit(solution)/shard_map/reduce_scatter | solution.py:40
  414.3 492.2 %copy-start.53 = (bf16[64,576]{0,1:T(8,128)(2,1)}, bf16[64,576]{0,1:T(8,128)(2,1)S(1)}, u32[]{:S(2)}) copy-start(bf16[64,576]{0,1:T(8,128)(2,1)S(1)} %slice.600) | copy-start | bytes 221188
  430.2 76.9 %all-gather.19.cloned.1.call-start = ((), (), s32[]{:S(2)}) async-start(), calls=%async_computation.25 | async-start | bytes 2088960 | tf_op jit(solution)/shard_map/all_gather | solution.py:36
  469.3 176.8 %reduce-scatter.17.cloned.1.call-start = ((), (), s32[]{:S(2)}) async-start(), calls=%async_computation.26 | async-start | bytes 2088960 | tf_op jit(solution)/shard_map/reduce_scatter | solution.py:40
  611.2 75.0 %all-gather.21.cloned.1.call-start = ((), (), s32[]{:S(2)}) async-start(), calls=%async_computation.27 | async-start | bytes 2088960 | tf_op jit(solution)/shard_map/all_gather | solution.py:36
  612.2 249.2 %copy-start.85 = (s32[272]{0:T(512)}, s32[272]{0:T(512)S(1)}, u32[]{:S(2)}) copy-start(s32[272]{0:T(512)S(1)} %fusion.167) | copy-start | bytes 3268
  647.3 214.1 %copy-start.83 = (f32[272]{0:T(512)}, f32[272]{0:T(512)S(1)}, u32[]{:S(2)}) copy-start(f32[272]{0:T(512)S(1)} %fusion.113) | copy-start | bytes 3268
  692.6 50.1 %slice-start.10 = ((s8[6684672]{0:T(1024)(128)(4,1)}), s8[4194304]{0:T(1024)(128)(4,1)S(1)}, s32[]{:S(2)}) async-start(s8[6684672]{0:T(1024)(128)(4,1)} %bitcast.429), calls=%async_computation.47 | async-start | bytes 8388608
  757.2 59.5 %all-to-all-start.5 = ((bf16[4,544,768]{2,1,0:T(8,128)(2,1)}), bf16[4,544,768]{2,1,0:T(8,128)(2,1)}, u32[]{:S(2)}, u32[]{:S(2)}) async-start(bf16[4,544,768]{2,1,0:T(8,128)(2,1)} %bitcast.374), calls=%async_computation.9 | async-start | bytes 6684672 | tf_op jit(solution)/shard_map/all_to_all | solution.py:46
  761.9 99.5 %reduce-scatter.19.cloned.1.call-start = ((), (), s32[]{:S(2)}) async-start(), calls=%async_computation.28 | async-start | bytes 2088960 | tf_op jit(solution)/shard_map/reduce_scatter | solution.py:40
  762.0 30.0 %collective-permute-start.4 = (bf16[768,768]{1,0:T(8,128)(2,1)}, bf16[768,768]{1,0:T(8,128)(2,1)S(1)}, u32[]{:S(2)}, u32[]{:S(2)}) collective-permute-start(bf16[768,768]{1,0:T(8,128)(2,1)} %get-tuple-element.35), channel_id=1, source_target_pairs={{0,16},{1,17},{2,18},{3,19},{4,20},{5,21},{6,22},{7,23},{8,24},{9,... | collective-permute-start | bytes 3538952 | tf_op jit(solution)/shard_map/ppermute | solution.py:54
  765.5 51.3 %collective-permute-start.5 = (bf16[768,768]{1,0:T(8,128)(2,1)}, bf16[768,768]{1,0:T(8,128)(2,1)}, u32[]{:S(2)}, u32[]{:S(2)}) collective-permute-start(bf16[768,768]{1,0:T(8,128)(2,1)} %get-tuple-element.36), channel_id=1, source_target_pairs={{0,16},{1,17},{2,18},{3,19},{4,20},{5,21},{6,22},{7,23},{8,24},{9,... | collective-permute-start | bytes 3538952 | tf_op jit(solution)/shard_map/ppermute | solution.py:54
  816.8 44.6 %copy-start.16 = (bf16[272,768]{1,0:T(8,128)(2,1)S(1)}, bf16[272,768]{1,0:T(8,128)(2,1)}, u32[]{:S(2)}) copy-start(bf16[272,768]{1,0:T(8,128)(2,1)} %reduce-scatter.15.cloned.1.call-done) | copy-start | bytes 1253380
  824.4 79.5 %all-gather.23.cloned.1.call-start = ((), (), s32[]{:S(2)}) async-start(), calls=%async_computation.29 | async-start | bytes 2088960 | tf_op jit(solution)/shard_map/all_gather | solution.py:36
  824.4 81.8 %copy-start.98 = (f32[272]{0:T(512)}, f32[272]{0:T(512)S(1)}, u32[]{:S(2)}) copy-start(f32[272]{0:T(512)S(1)} %neg.12) | copy-start | bytes 3268
  866.0 111.8 %reduce-scatter.21.cloned.1.call-start = ((), (), s32[]{:S(2)}) async-start(), calls=%async_computation.30 | async-start | bytes 2088960 | tf_op jit(solution)/shard_map/reduce_scatter | solution.py:40
  942.0 79.3 %copy-start.104 = (s32[1088]{0:T(1024)S(1)}, s32[1088]{0:T(1024)}, u32[]{:S(2)}) copy-start(s32[1088]{0:T(1024)} %copy-done.103) | copy-start | bytes 13060
  942.0 79.3 %all-gather.25.cloned.1.call-start = ((), (), s32[]{:S(2)}) async-start(), calls=%async_computation.31 | async-start | bytes 2088960 | tf_op jit(solution)/shard_map/all_gather | solution.py:36
  982.5 216.5 %copy-start.12 = (bf16[272,768]{1,0:T(8,128)(2,1)}, bf16[272,768]{1,0:T(8,128)(2,1)S(1)}, u32[]{:S(2)}) copy-start(bf16[272,768]{1,0:T(8,128)(2,1)S(1)} %get-tuple-element.104) | copy-start | bytes 1253380
  1027.7 50.1 %slice-start.8 = ((s8[6684672]{0:T(1024)(128)(4,1)}), s8[4194304]{0:T(1024)(128)(4,1)S(1)}, s32[]{:S(2)}) async-start(s8[6684672]{0:T(1024)(128)(4,1)} %bitcast.427), calls=%async_computation.45 | async-start | bytes 8388608
  1093.4 60.3 %all-to-all-start.7 = ((bf16[4,544,768]{2,1,0:T(8,128)(2,1)}), bf16[4,544,768]{2,1,0:T(8,128)(2,1)}, u32[]{:S(2)}, u32[]{:S(2)}) async-start(bf16[4,544,768]{2,1,0:T(8,128)(2,1)} %bitcast.375), calls=%async_computation.13 | async-start | bytes 6684672 | tf_op jit(solution)/shard_map/all_to_all | solution.py:46
  1098.1 98.4 %reduce-scatter.23.cloned.1.call-start = ((), (), s32[]{:S(2)}) async-start(), calls=%async_computation.32 | async-start | bytes 2088960 | tf_op jit(solution)/shard_map/reduce_scatter | solution.py:40
  1098.1 30.8 %collective-permute-start.6 = (bf16[768,768]{1,0:T(8,128)(2,1)S(1)}, bf16[768,768]{1,0:T(8,128)(2,1)}, u32[]{:S(2)}, u32[]{:S(2)}) collective-permute-start(bf16[768,768]{1,0:T(8,128)(2,1)S(1)} %get-tuple-element.39), channel_id=1, source_target_pairs={{16,0},{17,1},{18,2},{19,3},{20,4},{21,5},{22,6},{23,7},{24,8},{25... | collective-permute-start | bytes 3538952 | tf_op jit(solution)/shard_map/ppermute | solution.py:58
  1099.4 54.3 %collective-permute-start.7 = (bf16[768,768]{1,0:T(8,128)(2,1)S(1)}, bf16[768,768]{1,0:T(8,128)(2,1)}, u32[]{:S(2)}, u32[]{:S(2)}) collective-permute-start(bf16[768,768]{1,0:T(8,128)(2,1)S(1)} %get-tuple-element.40), channel_id=1, source_target_pairs={{16,0},{17,1},{18,2},{19,3},{20,4},{21,5},{22,6},{23,7},{24,8},{25... | collective-permute-start | bytes 3538952 | tf_op jit(solution)/shard_map/ppermute | solution.py:58
  1161.4 76.7 %all-gather.27.cloned.1.call-start = ((), (), s32[]{:S(2)}) async-start(), calls=%async_computation.33 | async-start | bytes 2088960 | tf_op jit(solution)/shard_map/all_gather | solution.py:36
  1161.5 44.0 %copy-start.61 = (f32[3,1024]{1,0:T(4,128)S(1)}, f32[3,1024]{1,0:T(4,128)}, u32[]{:S(2)}) copy-start(f32[3,1024]{1,0:T(4,128)} %copy-done.60) | copy-start | bytes 36868
  1200.2 131.7 %reduce-scatter.25.cloned.1.call-start = ((), (), s32[]{:S(2)}) async-start(), calls=%async_computation.34 | async-start | bytes 2088960 | tf_op jit(solution)/shard_map/reduce_scatter | solution.py:40
  1290.8 66.8 %reduce-scatter.29.cloned.1.call-start = ((), (), s32[]{:S(2)}) async-start(), calls=%async_computation.36 | async-start | bytes 1597440 | tf_op jit(solution)/shard_map/reduce_scatter | solution.py:454
  1322.3 61.4 %reduce-scatter.27.cloned.1.call-start = ((), (), s32[]{:S(2)}) async-start(), calls=%async_computation.35 | async-start | bytes 1597440 | tf_op jit(solution)/shard_map/reduce_scatter | solution.py:459
  1336.0 13.3 collective-permute-start.2
  1337.5 14.7 %collective-permute-start.3 = (bf16[272,768]{1,0:T(8,128)(2,1)S(1)}, bf16[272,768]{1,0:T(8,128)(2,1)S(1)}, u32[]{:S(2)}, u32[]{:S(2)}) collective-permute-start(bf16[272,768]{1,0:T(8,128)(2,1)S(1)} %copy-done.34), channel_id=1, source_target_pairs={{0,16},{1,17},{2,18},{3,19},{4,20},{5,21},{6,22},{7,23},{8,24},{9,... | collective-permute-start | bytes 1253384 | tf_op jit(solution)/shard_map/ppermute | solution.py:54
  1342.1 47.8 %collective-permute-start.9 = (bf16[272,768]{1,0:T(8,128)(2,1)S(1)}, bf16[272,768]{1,0:T(8,128)(2,1)}, u32[]{:S(2)}, u32[]{:S(2)}) collective-permute-start(bf16[272,768]{1,0:T(8,128)(2,1)S(1)} %copy-done.13), channel_id=1, source_target_pairs={{0,16},{1,17},{2,18},{3,19},{4,20},{5,21},{6,22},{7,23},{8,24},{9,... | collective-permute-start | bytes 1253384 | tf_op jit(solution)/shard_map/ppermute | solution.py:54
  1357.7 34.4 %collective-permute-start.11 = (bf16[1,208,768]{2,1,0:T(8,128)(2,1)}, bf16[1,208,768]{2,1,0:T(8,128)(2,1)S(1)}, u32[]{:S(2)}, u32[]{:S(2)}) collective-permute-start(bf16[1,208,768]{2,1,0:T(8,128)(2,1)} %reduce-scatter.29.cloned.1.call-done), channel_id=1, source_target_pairs={{0,16},{1,17},{2,18},{3,19},{4,20},{5,21},{6,22},{7,23},{8,24},{9,... | collective-permute-start | bytes 958472 | tf_op jit(solution)/shard_map/ppermute | solution.py:54
  1363.4 26.5 %collective-permute-start.8 = (bf16[272,768]{1,0:T(8,128)(2,1)}, bf16[272,768]{1,0:T(8,128)(2,1)S(1)}, u32[]{:S(2)}, u32[]{:S(2)}) collective-permute-start(bf16[272,768]{1,0:T(8,128)(2,1)} %fusion.111), channel_id=1, source_target_pairs={{16,0},{17,1},{18,2},{19,3},{20,4},{21,5},{22,6},{23,7},{24,8},{25... | collective-permute-start | bytes 1253384 | tf_op jit(solution)/shard_map/ppermute | solution.py:58
  1383.6 11.4 collective-permute-start.10
  (123 other events, 1838.4 us)
Sparse Core Ops, SparseCore 0:
  42.9 38.0 all-gather.10
  83.5 27.8 all-gather.12
  130.9 36.8 reduce-scatter.10
  171.2 37.7 all-gather.14
  335.6 34.7 reduce-scatter.12
  373.4 37.7 all-gather.16
  430.4 35.6 reduce-scatter.14
  469.4 37.7 all-gather.18
  611.3 34.7 reduce-scatter.16
  648.4 37.7 all-gather.20
  824.5 36.8 reduce-scatter.18
  866.2 37.7 all-gather.22
  942.2 35.6 reduce-scatter.20
  983.6 37.7 all-gather.24
  1161.5 34.9 reduce-scatter.22
  1200.3 37.7 all-gather.26
  1291.0 35.6 reduce-scatter.24
  1329.1 25.3 reduce-scatter.28
  1357.3 26.3 reduce-scatter.26
